TPU v7x, 128 devices: a whole 4x4x4 slice. The times are simulated.
128 devices in a mesh: grp: 4 (over x_lo, core), blk: 32 (over z, x_hi, y).
Axes of the slice: x: 4 (x_hi: 2, x_lo: 2; x = x_hi * 2 + x_lo), y: 4, z: 4, core: 2. Of those that a mesh axis runs over, the one named last changes fastest.
Arguments:
- head_vectors: float32 [32768, 256], P(('grp', 'blk')), may hold values from -6 to 6
- tail_vectors: float32 [32768, 256], P(('grp', 'blk')), may hold values from -6 to 6
- core_tensor: float32 [8192, 256], P(('grp', 'blk')), may hold values from -0.00390625 to 0.00390625
- core_moment: float32 [8192, 256], P(('grp', 'blk')), may hold values from -6 to 6
- core_second: float32 [8192, 256], P(('grp', 'blk')), may hold values from 0.5 to 2
- relation_table: float32 [1315, 32], replicated, may hold values from -6 to 6
- tile_relation: int32 [256, 8], P(('grp', 'blk')), may hold values from 0 to 1314
- positive_tail: int32 [32768, 4], P(('grp', 'blk')), may hold values from 0 to 255
- partner_table: int32 [32, 4, 4], P('blk'), may hold values from 0 to 3, as said below
Outputs:
- head_updated: float32 [32768, 256], P(('grp', 'blk'))
- tail_updated: float32 [32768, 256], P(('grp', 'blk'))
- head_losses: float32 [32768, 4], P(('grp', 'blk'))
- core_updated: float32 [8192, 256], P(('grp', 'blk'))
- moment_updated: float32 [8192, 256], P(('grp', 'blk'))
- second_updated: float32 [8192, 256], P(('grp', 'blk'))
- relation_grad: float32 [1315, 32], replicated
Inputs may be any that keep to these rules, and one draw needn't show every extreme that they name: partner_table[b, 0, g] = g; for every b, each row and each column of partner_table[b] holds every number 0 to 3 once.
All inputs are finite; a program needn't handle non-finite values.
Results may differ from a plain program's by a relative error of at most 0.0077.
Values may be sent and summed in bfloat16 or wider, within the bound.
No kernel may reach another device: no remote copies, remote signals or barrier semaphores. Data moves between devices by JAX's collectives and lax.ppermute only.
A program may use at most 128 MiB of HBM per device.

v0:
```python
import jax
import jax.numpy as jnp
from jax import lax
from jax.sharding import PartitionSpec as P

DE = 256
DR = 32
TILE = 128


entity_rate = 4.0
core_rate = 0.001
beta_first = 0.2
beta_second = 0.999


def train_pair(head_rows, tail_rows, core_low, relation_table, tile_ids, positive_col):
    head_count, width = head_rows.shape
    tail_count = tail_rows.shape[0]
    head_tiles = head_count // TILE
    tail_tiles = tail_count // TILE
    depth = core_low.shape[1] // width
    head_low = head_rows.astype(jnp.bfloat16)
    tail_low = tail_rows.astype(jnp.bfloat16)
    mixed_rows = jnp.dot(head_low, core_low, preferred_element_type=jnp.float32).astype(
        jnp.bfloat16
    )
    mixed_tiles = mixed_rows.reshape(head_tiles, TILE, depth, width)
    one_hot = (
        tile_ids.reshape(-1)[:, None]
        == jnp.arange(relation_table.shape[0], dtype=jnp.int32)[None, :]
    ).astype(jnp.float32)
    rel_vectors = (
        jnp.dot(one_hot, relation_table, precision=lax.Precision.HIGHEST)
        .reshape(head_tiles, tail_tiles, depth)
        .astype(jnp.bfloat16)
    )
    rel_core = jnp.einsum(
        "ihbc,ijb->ijhc", mixed_tiles, rel_vectors, preferred_element_type=jnp.float32
    ).astype(jnp.bfloat16)
    tail_tiled = tail_low.reshape(tail_tiles, TILE, width)
    scores = jnp.einsum(
        "ijhc,jtc->ihjt", rel_core, tail_tiled, preferred_element_type=jnp.float32
    ).reshape(head_count, tail_count)
    is_positive = jnp.arange(tail_count, dtype=jnp.int32)[None, :] == positive_col[:, None]
    pair_loss = jnp.where(
        is_positive, jax.nn.softplus(-scores), jax.nn.softplus(scores) / tail_count
    )
    row_loss = jnp.sum(pair_loss, axis=1)
    slope_low = jnp.where(
        is_positive, -jax.nn.sigmoid(-scores), jax.nn.sigmoid(scores) / tail_count
    ).astype(jnp.bfloat16)
    slope_tiles = slope_low.reshape(head_tiles, TILE, tail_tiles, TILE)
    grad_relcore = jnp.einsum(
        "ihjt,jtc->ijhc", slope_tiles, tail_tiled, preferred_element_type=jnp.float32
    ).astype(jnp.bfloat16)
    grad_tail = jnp.einsum(
        "ihjt,ijhc->jtc", slope_tiles, rel_core, preferred_element_type=jnp.float32
    ).reshape(tail_count, width)
    grad_relvec = jnp.einsum(
        "ijhc,ihbc->ijb", grad_relcore, mixed_tiles, preferred_element_type=jnp.float32
    )
    grad_mixed = (
        jnp.einsum("ijhc,ijb->ihbc", grad_relcore, rel_vectors, preferred_element_type=jnp.float32)
        .reshape(head_count, depth * width)
        .astype(jnp.bfloat16)
    )
    grad_head = lax.dot_general(
        grad_mixed, core_low, (((1,), (1,)), ((), ())), preferred_element_type=jnp.float32
    )
    grad_core = lax.dot_general(
        head_low, grad_mixed, (((0,), (0,)), ((), ())), preferred_element_type=jnp.float32
    )
    grad_relation = jnp.dot(
        one_hot.T, grad_relvec.reshape(-1, depth), precision=lax.Precision.HIGHEST
    )
    return (
        head_rows - entity_rate * grad_head,
        tail_rows - entity_rate * grad_tail,
        grad_core,
        grad_relation,
        row_loss,
    )


def holder(table_row, value):
    return jnp.sum(
        jnp.arange(table_row.shape[0], dtype=jnp.int32) * (table_row == value).astype(jnp.int32)
    )


def body(
    head_vectors,
    tail_vectors,
    core_tensor,
    core_moment,
    core_second,
    relation_table,
    tile_relation,
    positive_tail,
    partner_table,
):
    buckets = lax.axis_size("grp")
    member = lax.axis_index("grp")
    table = partner_table[0]
    core_low = lax.all_gather(
        core_tensor.astype(jnp.bfloat16), ("grp", "blk"), axis=0, tiled=True
    ).reshape(DE, DR * DE)
    tail_count = tail_vectors.shape[0]
    tail_tiles = tail_count // TILE
    whole_total = jnp.zeros((DE, DR * DE), jnp.float32)
    relation_sum = jnp.zeros(relation_table.shape, jnp.float32)
    head_now = head_vectors
    tail_now = tail_vectors
    loss_columns = []
    for round_index in range(buckets):
        partition = table[round_index, member]
        tile_ids = lax.dynamic_slice_in_dim(tile_relation, partition * tail_tiles, tail_tiles, 1)
        positive_col = lax.dynamic_slice_in_dim(positive_tail, partition, 1, 1)[:, 0]
        head_now, tail_now, grad_core, grad_relation, row_loss = train_pair(
            head_now, tail_now, core_low, relation_table, tile_ids, positive_col
        )
        whole_total = whole_total + grad_core
        relation_sum = relation_sum + grad_relation
        loss_columns.append(row_loss)
        if round_index + 1 < buckets:
            target = table[round_index + 1, member]
        else:
            target = member
        source = holder(table[round_index], target)
        gathered = lax.all_gather(tail_now, "grp", axis=0, tiled=True)
        tail_now = lax.dynamic_slice_in_dim(gathered, source * tail_count, tail_count, 0)
    loss_now = jnp.stack(loss_columns, axis=1)
    entry_count = DE * DR * DE
    own_grad = lax.psum_scatter(
        whole_total.reshape(-1, DE), ("grp", "blk"), scatter_dimension=0, tiled=True
    )
    relation_grad, square_sum = lax.psum(
        (relation_sum, jnp.sum(own_grad * own_grad)), ("grp", "blk")
    )
    mean_square = square_sum / entry_count
    normalized = own_grad / jnp.sqrt(mean_square + 1e-06)
    moment_updated = beta_first * core_moment + (1.0 - beta_first) * normalized
    second_updated = beta_second * core_second + (1.0 - beta_second) * normalized * normalized
    core_updated = core_tensor - core_rate * moment_updated / (jnp.sqrt(second_updated) + 1e-08)
    return (
        head_now,
        tail_now,
        loss_now,
        core_updated,
        moment_updated,
        second_updated,
        relation_grad,
    )


def solution(mesh):
    return jax.shard_map(
        body,
        mesh=mesh,
        in_specs=(
            P(("grp", "blk"), None),
            P(("grp", "blk"), None),
            P(("grp", "blk"), None),
            P(("grp", "blk"), None),
            P(("grp", "blk"), None),
            P(),
            P(("grp", "blk"), None),
            P(("grp", "blk"), None),
            P("blk", None, None),
        ),
        out_specs=(
            P(("grp", "blk"), None),
            P(("grp", "blk"), None),
            P(("grp", "blk"), None),
            P(("grp", "blk"), None),
            P(("grp", "blk"), None),
            P(("grp", "blk"), None),
            P(),
        ),
        check_vma=False,
    )
```

profile of v0, /device:TPU:1, one launch (start us, length us, event | category | flops | bytes accessed | tf_op | source)
XLA Modules:
  0.0 1293.1 jit_solution(7316451642557518568)
XLA Ops:
  7.2 1.5 convert_element_type.170
  8.8 1.4 constant_dynamic-slice_fusion.3
  18.0 3.5 fusion.95
  23.5 0.9 constant_dynamic-slice_fusion.2
  24.8 1.0 convert_element_type.173
  28.4 0.9 constant_dynamic-slice_fusion.1
  30.2 290.2 %all-gather.6.cloned.1.call-done = bf16[8192,256]{1,0:T(8,128)(2,1)} async-done(((bf16[64,256]{1,0:T(8,128)(2,1)}), bf16[8192,256]{1,0:T(8,128)(2,1)}) %all-gather.6.cloned.1.call-update) | async-done | bytes 4194320 | tf_op jit(solution)/shard_map/all_gather | solution.py:106
  320.4 7.4 reshape.202
  327.8 3.4 convolution_convert_fusion.3
  331.3 1.4 copy.121
  332.7 0.7 fusion.16
  334.7 0.7 bitcast_subtract_fusion.3
  335.7 1.3 convolution_convert_fusion.7
  337.0 4.4 copy.122
  341.4 1.3 fusion.36
  342.6 1.3 convolution_convert_fusion.2
  343.9 1.4 copy.123
  345.3 2.0 copy-done.6
  347.3 0.7 fusion.19
  347.9 4.6 convolution_bitcast_fusion
  352.5 4.8 all-gather.8.cloned.1.call-done
  357.3 1.0 dynamic-slice_convert_fusion.2
  359.2 1.7 bitcast_subtract_fusion.2
  361.5 1.3 convolution_convert_fusion.6
  362.9 4.4 copy.124
  367.2 1.3 fusion.37
  368.5 1.3 convolution_convert_fusion.1
  369.8 1.4 copy.125
  371.2 1.9 copy-done.8
  373.8 5.0 convolution_add_fusion.2
  378.9 3.8 all-gather.10.cloned.1.call-done
  382.7 1.0 dynamic-slice_convert_fusion.1
  384.7 1.7 bitcast_subtract_fusion.1
  386.7 1.3 convolution_convert_fusion.5
  388.0 4.4 copy.126
  392.4 1.3 fusion.38
  393.7 1.3 convolution_convert_fusion
  395.0 1.4 copy.127
  396.4 2.0 copy-done.9
  399.1 5.0 convolution_add_fusion.1
  404.1 4.1 all-gather.12.cloned.1.call-done
  408.2 1.0 dynamic-slice_convert_fusion
  409.2 1.7 fusion.41
  411.4 1.3 convolution_convert_fusion.4
  412.7 4.3 copy.128
  417.0 2.0 copy-done.11
  419.0 8.4 convolution_add_fusion
  427.4 9.0 copy.68
  436.4 9.3 reshape.211
  446.7 3.5 fusion.12
  450.5 1.2 fusion.8
  452.4 1.7 bitcast_subtract_fusion
  454.2 3.6 fusion.4
  458.1 1.2 fusion
  459.3 1.0 convolution_add_fusion.3
  460.3 5.5 fusion.39
  466.5 650.5 %reduce-scatter.2.cloned.1.call-done = f32[64,256]{1,0:T(8,128)} async-done(((f32[8192,256]{1,0:T(8,128)}), f32[64,256]{1,0:T(8,128)}) %reduce-scatter.2.cloned.1.call-update) | async-done | bytes 65552 | tf_op jit(solution)/shard_map/reduce_scatter | solution.py:135
  1117.0 1.5 multiply_reduce_fusion
  1118.4 16.6 %all-gather.14.cloned.1.call-done = f32[1024,256]{1,0:T(8,128)} async-done(((f32[256,256]{1,0:T(8,128)}), f32[1024,256]{1,0:T(8,128)}) %all-gather.14.cloned.1.call-update) | async-done | bytes 1048592 | tf_op jit(solution)/shard_map/all_gather | solution.py:131
  1135.0 1.7 constant_dynamic-slice_fusion
  1136.7 66.2 %psum.14 = f32[]{:T(128)} all-reduce(f32[]{:T(128)} %multiply_reduce_fusion), channel_id=1, replica_groups=mesh['grp'=4,'blk'=32] {'grp','blk'}, use_global_device_ids=true, to_apply=%region_10.11 | all-reduce | flops 1 | bytes 8 | tf_op jit(solution)/shard_map/psum | solution.py:138
  1203.6 1.5 divide_subtract_fusion
  1205.2 79.2 %all-reduce.2.cloned.1.call-done = f32[1315,32]{0,1:T(8,128)} async-done(((f32[1315,32]{0,1:T(8,128)}), f32[1315,32]{0,1:T(8,128)}) %all-reduce.2.cloned.1.call-update) | async-done | bytes 168336 | tf_op jit(solution)/shard_map/psum | solution.py:138
  1284.4 1.6 copy.152
  (83 shorter events, 10.0 us)
Async XLA Ops:
  7.2 22.0 %copy-start = (f32[1315,32]{0,1:T(8,128)S(1)}, f32[1315,32]{0,1:T(8,128)}, u32[]{:S(2)}) copy-start(f32[1315,32]{0,1:T(8,128)} %param.14) | copy-start | bytes 504964
  7.2 313.2 %all-gather.6.cloned.1.call-start = ((), (), s32[]{:S(2)}) async-start(), calls=%async_computation.1 | async-start | bytes 4227072 | tf_op jit(solution)/shard_map/all_gather | solution.py:106
  8.7 348.6 %all-gather.8.cloned.1.call-start = ((), (), s32[]{:S(2)}) async-start(), calls=%async_computation.2 | async-start | bytes 1310720 | tf_op jit(solution)/shard_map/all_gather | solution.py:131
  30.2 297.7 %copy-start.13 = (f32[256,256]{1,0:T(8,128)S(1)}, f32[256,256]{1,0:T(8,128)}, u32[]{:S(2)}) copy-start(f32[256,256]{1,0:T(8,128)} %param.9) | copy-start | bytes 786436
  332.7 2.0 copy-start.5
  332.7 2.0 copy-start.12
  335.4 47.2 %all-gather.10.cloned.1.call-start = ((), (), s32[]{:S(2)}) async-start(), calls=%async_computation.3 | async-start | bytes 1310720 | tf_op jit(solution)/shard_map/all_gather | solution.py:131
  337.0 4.4 copy-start.2
  345.3 2.0 copy-start.6
  360.9 47.3 %all-gather.12.cloned.1.call-start = ((), (), s32[]{:S(2)}) async-start(), calls=%async_computation.4 | async-start | bytes 1310720 | tf_op jit(solution)/shard_map/all_gather | solution.py:131
  362.9 4.4 copy-start.3
  368.5 5.3 slice-start
  369.8 4.0 slice-start.1
  371.2 2.0 copy-start.8
  386.4 730.5 %reduce-scatter.2.cloned.1.call-start = ((), (), s32[]{:S(2)}) async-start(), calls=%async_computation.6 | async-start | bytes 8454144 | tf_op jit(solution)/shard_map/reduce_scatter | solution.py:135
  388.0 4.4 copy-start.4
  393.7 5.4 slice-start.2
  395.0 4.1 slice-start.3
  396.3 2.1 copy-start.9
  417.0 2.0 copy-start.11
  445.7 689.3 %all-gather.14.cloned.1.call-start = ((), (), s32[]{:S(2)}) async-start(), calls=%async_computation.5 | async-start | bytes 1310720 | tf_op jit(solution)/shard_map/all_gather | solution.py:131
  446.7 3.9 copy-start.7
  454.1 830.3 %all-reduce.2.cloned.1.call-start = ((), (), s32[]{:S(2)}) async-start(), calls=%async_computation.7 | async-start | bytes 360448 | tf_op jit(solution)/shard_map/psum | solution.py:138
  454.2 3.9 copy-start.10
  460.3 825.7 %copy-start.1 = (f32[1315,32]{0,1:T(8,128)S(1)}, f32[1315,32]{0,1:T(8,128)}, u32[]{:S(2)}) copy-start(f32[1315,32]{0,1:T(8,128)} %param.14) | copy-start | bytes 504964
  460.3 743.3 %copy-start.14 = (f32[64,256]{1,0:T(8,128)S(1)}, f32[64,256]{1,0:T(8,128)}, u32[]{:S(2)}) copy-start(f32[64,256]{1,0:T(8,128)} %param.11) | copy-start | bytes 196612
  460.3 743.3 %copy-start.15 = (f32[64,256]{1,0:T(8,128)S(1)}, f32[64,256]{1,0:T(8,128)}, u32[]{:S(2)}) copy-start(f32[64,256]{1,0:T(8,128)} %param.12) | copy-start | bytes 196612
  460.3 743.3 %copy-start.16 = (f32[64,256]{1,0:T(8,128)S(1)}, f32[64,256]{1,0:T(8,128)}, u32[]{:S(2)}) copy-start(f32[64,256]{1,0:T(8,128)} %param.13) | copy-start | bytes 196612
Sparse Core Ops, SparseCore 0:
  10.3 310.0 all-gather.5
  335.6 21.7 all-gather.7
  361.0 21.6 all-gather.9
  386.6 21.6 all-gather.11
  445.8 671.1 reduce-scatter.1
  1119.2 15.7 all-gather.13
  1141.0 143.3 all-reduce.1
where the time goes:
time: 1300 us; the launch traced here: 1290 us
  waiting for transfers between devices  1050 us (81%)
  local copies, waits for them, and re-layouts  67.2 us (5%)
  blocking collectives  66.2 us (5%)
  matrix products  65.1 us (5%)
  between operations  28.7 us (2%)
  other arithmetic  15.4 us (1%)
    reduce_scatter x1, waiting for transfers between devices, body(): lax.psum_scatter(whole_total.reshape(-1, DE), ('grp', 'blk'), scatter_dim...  651 us
    all_gather x1, waiting for transfers between devices, body(): lax.all_gather(core_tensor.astype(jnp.bfloat16), ('grp', 'blk'), axis=0,...  290 us
    psum x1, waiting for transfers between devices, body(): lax.psum((relation_sum, jnp.sum(own_grad * own_grad)), ('grp', 'blk'))  79.2 us
    psum x1, blocking collectives, body(): lax.psum((relation_sum, jnp.sum(own_grad * own_grad)), ('grp', 'blk'))  66.2 us
    unnamed x51, local copies, waits for them, and re-layouts  32.8 us
    all_gather x4, waiting for transfers between devices, body(): gathered = lax.all_gather(tail_now, 'grp', axis=0, tiled=True)  29.3 us
  transfers between devices with their start and end apart: 7, of which 7 were waited for; matrix products, arithmetic and copies ran while one was open for 6% of the time, Pallas kernels for 0%

commit v1 on v0

v1 whole, which is shorter than its diff:
```python
import jax
import jax.numpy as jnp
from jax import lax
from jax.experimental import pallas as pl
from jax.experimental.pallas import tpu as pltpu
from jax.sharding import Mesh, PartitionSpec as P

DE = 256
DR = 32
TILE = 128
GROUP = 4
PAIR_ROWS = 64
REL_PAD = 1408

entity_rate = 4.0
core_rate = 0.001
beta_first = 0.2
beta_second = 0.999

AXES = ("xl", "co", "z", "xh", "y")
MEMBERS = ("xl", "co")
GROUPS = ("z", "xh", "y")
CHIPS = ("xl", "z", "xh", "y")

f32 = jnp.float32
bf16 = jnp.bfloat16


def mm(a, b):
    return jnp.dot(a, b, preferred_element_type=f32)


def mm_nt(a, b):
    return lax.dot_general(a, b, (((1,), (1,)), ((), ())), preferred_element_type=f32)


def mm_tn(a, b):
    return lax.dot_general(a, b, (((0,), (0,)), ((), ())), preferred_element_type=f32)


def train_kernel(
    meta,
    mine,
    other,
    d0,
    d1,
    d2,
    d3,
    table,
    out_head,
    out_tail,
    out_loss,
    out_pay,
    rel_rows,
    id_rows,
    spread,
    spread_t,
    cores,
    grads,
    heads,
    heads_low,
    tails,
    tails_low,
    tail_grads,
):
    member = meta[0]
    co = meta[1]
    xl = meta[2]
    given = (d0, d1, d2, d3)

    for s in range(GROUP):
        for i in range(2):
            for t in range(GROUP):
                for j in range(2):
                    n = ((s * 2 + i) * GROUP + t) * 2 + j
                    rid = meta[19 + s * 16 + i * 8 + (t ^ member) * 2 + j]
                    rel_rows[n : n + 1, :] = table[pl.ds(rid, 1), :]
                    id_rows[n : n + 1, :] = jnp.full((1, 128), rid.astype(f32))

    rel_low = rel_rows[...].astype(bf16)
    copies = (
        lax.broadcasted_iota(jnp.int32, (DR, 256), 1) % DR
        == lax.broadcasted_iota(jnp.int32, (DR, 256), 0)
    ).astype(bf16)
    rel_wide = mm(rel_low, copies)
    on_row = (
        lax.broadcasted_iota(jnp.int32, (64, 8, 256), 2) // DR
        == lax.broadcasted_iota(jnp.int32, (64, 8, 256), 1)
    )
    spread_f = jnp.where(on_row, rel_wide[:, None, :], 0.0).reshape(512, 256)
    spread[...] = spread_f.astype(bf16)
    spread_t[...] = spread_f.T.astype(bf16)

    def core_step(q, carry):
        for src, side in ((mine, co), (other, 1 - co)):
            row = pl.multiple_of(q * 512, 512)
            parts = [
                mm(spread[...], src[pl.ds(row + 256 * e, 256), :]).reshape(64, 8, 256)
                for e in range(2)
            ]
            at = 64 * (2 * (q // 4) + side) + 16 * (q % 4)
            cores[:, pl.ds(pl.multiple_of(at, 16), 16), :] = jnp.concatenate(
                parts, axis=1
            ).astype(bf16)
        return carry

    lax.fori_loop(0, 8, core_step, 0)

    for s in range(GROUP):
        heads[s] = given[s][:, 0:256]
        tails[s] = given[s][:, 256:512]

    lane = lax.broadcasted_iota(jnp.int32, (TILE, TILE), 1)
    half = pl.multiple_of((member // 2) * 128, 128)
    odd = member % 2 == 1

    def round_step(k, carry):
        slots = [meta[3 + k * GROUP + (member ^ s)] ^ member for s in range(GROUP)]
        for s in range(GROUP):
            tails_low[s] = tails[slots[s]].astype(bf16)
            heads_low[s] = heads[s].astype(bf16)
        for s in range(GROUP):
            t = slots[s]
            own = meta[3 + k * GROUP + (member ^ s)]
            extra = given[s][:, 512:640]
            column = lax.broadcasted_iota(jnp.int32, (256, 128), 1) == own
            positive = jnp.sum(jnp.where(column, extra, 0.0), axis=1, keepdims=True).astype(
                jnp.int32
            )
            for i in range(2):
                rows = slice(TILE * i, TILE * i + TILE)
                head_low = heads_low[s, rows, :]
                head_part = heads_low[s, rows, pl.ds(half, 128)]
                grad_head = None
                row_loss = None
                for j in range(2):
                    cols = slice(TILE * j, TILE * j + TILE)
                    n = ((s * 2 + i) * GROUP + t) * 2 + j
                    core = cores[n]
                    tail_low = tails_low[s, cols, :]
                    rel_core = mm(head_low, core).astype(bf16)
                    score = mm_nt(rel_core, tail_low)
                    hit = lane + TILE * j == positive[rows]
                    signed = jnp.where(hit, -score, score)
                    slope = (
                        jax.nn.sigmoid(signed) * jnp.where(hit, -1.0, 1.0 / 256.0)
                    ).astype(bf16)
                    if s == 0:
                        part = jnp.sum(
                            (
                                jnp.maximum(signed, 0.0)
                                + jnp.log1p(jnp.exp(-jnp.abs(signed)))
                            )
                            * jnp.where(hit, 1.0, 1.0 / 256.0),
                            axis=1,
                            keepdims=True,
                        )
                        row_loss = part if row_loss is None else row_loss + part
                    grad_relcore = mm(slope, tail_low).astype(bf16)
                    grad_tail = mm_tn(slope, rel_core)
                    if i == 0:
                        tail_grads[s, cols, :] = grad_tail
                    else:
                        tail_grads[s, cols, :] += grad_tail
                    more = mm_nt(grad_relcore, core)
                    grad_head = more if grad_head is None else grad_head + more
                    outer = mm_tn(head_part, grad_relcore)
                    grads[n] = jnp.where(odd, outer[64:], outer[:64])
                heads[s, rows, :] -= entity_rate * grad_head
                if s == 0:
                    place = lax.broadcasted_iota(jnp.int32, (TILE, GROUP), 1) == k
                    out_loss[rows, :] = jnp.where(place, row_loss, out_loss[rows, :])
        for s in range(GROUP):
            tails[slots[s]] -= entity_rate * tail_grads[s]
        return carry

    out_loss[...] = jnp.zeros_like(out_loss)
    lax.fori_loop(0, GROUP, round_step, 0)
    out_head[...] = heads[0]
    out_tail[...] = tails[0]

    total = jnp.zeros((512, 256), f32)
    for e in range(8):
        low = grads[:, 8 * e : 8 * e + 8, :].reshape(512, 256).astype(bf16)
        part = mm(spread_t[...], low).astype(bf16)
        for d in range(4):
            out_pay[4 * e + d, 0:64, :] = part[64 * d : 64 * d + 64, :]
        own_core = mine[pl.ds(pl.multiple_of(xl * 2048 + 256 * e, 256), 256), :]
        total = total + mm_nt(low, own_core)
    wide = jnp.sum(jnp.where(on_row, total.reshape(64, 8, 256), 0.0), axis=1)
    folded = wide[:, :128] + wide[:, 128:]
    folded = folded + pltpu.roll(folded, 64, 1)
    folded = folded + pltpu.roll(folded, 32, 1)
    lanes = lax.broadcasted_iota(jnp.int32, (16, 128), 1)
    packed = jnp.zeros((16, 128), f32)
    names = jnp.zeros((16, 128), f32)
    for q in range(4):
        ids = id_rows[16 * q : 16 * q + 16, :]
        high = jnp.floor(ids * (1.0 / 256.0))
        rest = ids - 256.0 * high
        packed = jnp.where(lanes // 32 == q, folded[16 * q : 16 * q + 16, :], packed)
        names = jnp.where(lanes == 32 * q, high, jnp.where(lanes == 32 * q + 1, rest, names))
    tag = jnp.concatenate([packed, names], axis=1).astype(bf16)
    for d in range(32):
        out_pay[d, 64:80, :] = tag


def sum_kernel(got, out_grad, out_square, out_rel):
    total = got[0, 0:64, :].astype(f32)
    for d in range(1, 32):
        total = total + got[d, 0:64, :].astype(f32)
    out_grad[...] = total
    out_square[...] = jnp.full((128, 128), jnp.sum(total * total))
    tags = got[:, 64:80, :].reshape(512, 256)
    values = tags[:, :128]
    names = tags[:, 128:].astype(f32)
    for e in range(REL_PAD // 128):
        lane = (lax.broadcasted_iota(jnp.int32, (512, 128), 1) + 128 * e).astype(f32)
        out = jnp.zeros((DR, 128), f32)
        for q in range(4):
            rid = names[:, 32 * q : 32 * q + 1] * 256.0 + names[:, 32 * q + 1 : 32 * q + 2]
            hot = (lane == rid).astype(f32).astype(bf16)
            out = out + mm_tn(values, hot)[32 * q : 32 * q + 32, :]
        out_rel[:, 128 * e : 128 * e + 128] = out


def adam_kernel(
    squares, own, core, moment, second, r0, r1, r2, r3, out_core, out_moment, out_second, out_rel
):
    mean_square = jnp.sum(squares[...]) * (1.0 / 128.0 / (DE * DR * DE))
    scale = jnp.full((1, 1), mean_square) + 1e-06
    normalized = own[...] / jnp.sqrt(scale)
    moment_updated = beta_first * moment[...] + (1.0 - beta_first) * normalized
    second_updated = beta_second * second[...] + (1.0 - beta_second) * normalized * normalized
    out_moment[...] = moment_updated
    out_second[...] = second_updated
    out_core[...] = core[...] - core_rate * moment_updated / (jnp.sqrt(second_updated) + 1e-08)
    out_rel[...] = (r0[...] + r1[...]) + (r2[...] + r3[...])


def exchange(value, axes, step):
    size = lax.axis_size(axes)
    return lax.ppermute(value, axes, [(i, i ^ step) for i in range(size)])


def vmem(count):
    return [pl.BlockSpec(memory_space=pltpu.VMEM)] * count


def body(
    head_vectors,
    tail_vectors,
    core_tensor,
    core_moment,
    core_second,
    relation_table,
    tile_relation,
    positive_tail,
    partner_table,
):
    member = lax.axis_index(MEMBERS)
    co = lax.axis_index("co")
    xl = lax.axis_index("xl")
    rel_count = relation_table.shape[0]

    extra = jnp.zeros((256, 128), f32)
    extra = extra.at[:, 0:4].set(positive_tail.astype(f32))
    extra = extra.at[0:2, 8:16].set(tile_relation.astype(f32))
    own = jnp.concatenate([head_vectors, tail_vectors, extra], axis=1)
    group = [own] + [exchange(own, MEMBERS, s) for s in range(1, GROUP)]

    low = core_tensor.astype(bf16)
    mine = lax.all_to_all(
        jnp.broadcast_to(low[None], (64, 64, DE)), CHIPS, split_axis=0, concat_axis=0, tiled=True
    ).reshape(4096, DE)
    other = exchange(mine, "co", 1)

    ids = jnp.concatenate([g[0:2, 520:528].reshape(-1) for g in group]).astype(jnp.int32)
    meta = jnp.concatenate(
        [jnp.stack([member, co, xl]).astype(jnp.int32), partner_table.reshape(-1), ids]
    )
    head_now, tail_now, loss_now, pay = pl.pallas_call(
        train_kernel,
        out_shape=(
            jax.ShapeDtypeStruct((256, DE), f32),
            jax.ShapeDtypeStruct((256, DE), f32),
            jax.ShapeDtypeStruct((256, GROUP), f32),
            jax.ShapeDtypeStruct((32, 80, DE), bf16),
        ),
        in_specs=[pl.BlockSpec(memory_space=pltpu.SMEM)] + vmem(7),
        out_specs=tuple(vmem(4)),
        scratch_shapes=[
            pltpu.VMEM((64, DR), f32),
            pltpu.VMEM((64, 128), f32),
            pltpu.VMEM((512, 256), bf16),
            pltpu.VMEM((256, 512), bf16),
            pltpu.VMEM((64, 256, 256), bf16),
            pltpu.VMEM((64, 64, 256), f32),
            pltpu.VMEM((GROUP, 256, DE), f32),
            pltpu.VMEM((GROUP, 256, DE), bf16),
            pltpu.VMEM((GROUP, 256, DE), f32),
            pltpu.VMEM((GROUP, 256, DE), bf16),
            pltpu.VMEM((GROUP, 256, DE), f32),
        ],
        compiler_params=pltpu.CompilerParams(vmem_limit_bytes=48 * 1024 * 1024),
    )(meta, mine, other, *group, relation_table)

    got = lax.all_to_all(pay, GROUPS, split_axis=0, concat_axis=0, tiled=True)
    own_grad, square, rel_part = pl.pallas_call(
        sum_kernel,
        out_shape=(
            jax.ShapeDtypeStruct((64, DE), f32),
            jax.ShapeDtypeStruct((128, 128), f32),
            jax.ShapeDtypeStruct((DR, REL_PAD), f32),
        ),
        in_specs=vmem(1),
        out_specs=tuple(vmem(3)),
        compiler_params=pltpu.CompilerParams(vmem_limit_bytes=32 * 1024 * 1024),
    )(got)
    rel_parts = [rel_part] + [exchange(rel_part, MEMBERS, s) for s in range(1, GROUP)]
    squares = lax.all_to_all(square, AXES, split_axis=0, concat_axis=0, tiled=True)
    core_updated, moment_updated, second_updated, rel_sum = pl.pallas_call(
        adam_kernel,
        out_shape=(
            jax.ShapeDtypeStruct((64, DE), f32),
            jax.ShapeDtypeStruct((64, DE), f32),
            jax.ShapeDtypeStruct((64, DE), f32),
            jax.ShapeDtypeStruct((DR, REL_PAD), f32),
        ),
        in_specs=vmem(9),
        out_specs=tuple(vmem(4)),
        compiler_params=pltpu.CompilerParams(vmem_limit_bytes=32 * 1024 * 1024),
    )(squares, own_grad, core_tensor, core_moment, core_second, *rel_parts)
    return (
        head_now,
        tail_now,
        loss_now,
        core_updated,
        moment_updated,
        second_updated,
        rel_sum[:, :rel_count].T,
    )


def solution(mesh):
    fine = Mesh(mesh.devices.reshape(2, 2, 4, 2, 4), AXES)
    rows = P(AXES, None)
    return jax.shard_map(
        body,
        mesh=fine,
        in_specs=(rows, rows, rows, rows, rows, P(), rows, rows, P(GROUPS, None, None)),
        out_specs=(rows, rows, rows, rows, rows, rows, P()),
        check_vma=False,
    )
```

time: 1300 us -> 165 us (0.13)
  waiting for transfers between devices: 1050 us -> 36.4 us
  matrix products: 65.1 us -> 0 us
  local copies, waits for them, and re-layouts: 67.2 us -> 5.24 us
  Pallas kernels: 0 us -> 37.7 us
  between operations: 28.7 us -> 0.82 us
    reduce_scatter x1 -> x0, waiting for transfers between devices: 651 us -> none  [body(): lax.psum_scatter(whole_total.reshape(-1, DE), ('grp', 'blk'), scatter_dim...]
    all_gather x5 -> x0, waiting for transfers between devices: 320 us -> none  [the longest x1 290 us: body(): lax.all_gather(core_tensor.astype(jnp.bfloat16), ('grp', 'blk'), axis=0,...]
    psum x1 -> x0, waiting for transfers between devices: 79.2 us -> none  [body(): lax.psum((relation_sum, jnp.sum(own_grad * own_grad)), ('grp', 'blk'))]
    all_to_all x0 -> x2, blocking collectives: none -> 67 us  [the longest x1 39.6 us: body(): lax.all_to_all(jnp.broadcast_to(low[None], (64, 64, DE)), CHIPS, split_ax...]
    psum x1 -> x0, blocking collectives: 66.2 us -> none  [body(): lax.psum((relation_sum, jnp.sum(own_grad * own_grad)), ('grp', 'blk'))]
    dot_general x44 -> x0, matrix products: 65.1 us -> none  [the longest x4 23 us: train_pair(): lax.dot_general(head_low, grad_mixed, (((0,), (0,)), ((), ())), preferred...]
    pallas_call x0 -> x3, Pallas kernels: none -> 37.7 us  [the longest x1 34.1 us: body(): pl.pallas_call(train_kernel, out_shape=(jax.ShapeDtypeStruct((256, DE), f...]
    unnamed x51 -> x22, local copies, waits for them, and re-layouts: 32.8 us -> 0.96 us
  transfers between devices with their start and end apart: 7 -> 8, of which waited for: 7 -> 3; matrix products, arithmetic and copies ran while one was open for 6% -> 5% of each run, Pallas kernels for 0% -> 0%
where the time goes in v1:
time: 165 us; the launch traced here: 164 us
  blocking collectives  67 us (41%)
  Pallas kernels  37.7 us (23%)
  waiting for transfers between devices  36.4 us (22%)
  starting transfers between devices  12.1 us (7%)
  local copies, waits for them, and re-layouts  5.24 us (3%)
  other arithmetic  4.94 us (3%)
    all_to_all x1, blocking collectives, body(): lax.all_to_all(jnp.broadcast_to(low[None], (64, 64, DE)), CHIPS, split_ax...  39.6 us
    pallas_call x1, Pallas kernels, body(): pl.pallas_call(train_kernel, out_shape=(jax.ShapeDtypeStruct((256, DE), f...  34.1 us
    all_to_all x1, blocking collectives, body(): got = lax.all_to_all(pay, GROUPS, split_axis=0, concat_axis=0, tiled=True)  27.4 us
    ppermute x7, waiting for transfers between devices, exchange(): return lax.ppermute(value, axes, [(i, i ^ step) for i in range(size)])  27.3 us
    all_to_all x1, waiting for transfers between devices, body(): lax.all_to_all(square, AXES, split_axis=0, concat_axis=0, tiled=True)  9.13 us
    ppermute x7, starting transfers between devices, exchange(): return lax.ppermute(value, axes, [(i, i ^ step) for i in range(size)])  8.25 us
    another operation x5, other arithmetic  3.96 us
    all_to_all x1, starting transfers between devices, body(): lax.all_to_all(square, AXES, split_axis=0, concat_axis=0, tiled=True)  3.89 us
  transfers between devices with their start and end apart: 8, of which 3 were waited for; matrix products, arithmetic and copies ran while one was open for 5% of the time, Pallas kernels for 0%

profile of v1, /device:TPU:1, one launch (start us, length us, event | category | flops | bytes accessed | tf_op | source)
XLA Modules:
  0.0 164.2 jit_solution(5048815402591690611)
XLA Ops:
  0.6 0.8 convert_element_type.15
  1.5 0.2 broadcast_in_dim.2
  1.7 0.0 copy-start.6
  1.7 0.0 copy-start.9
  1.8 0.0 copy-start.8
  1.8 0.0 copy-start.3
  1.8 0.0 copy-start.4
  1.8 39.6 %all_to_all.21 = bf16[64,64,256]{2,1,0:T(8,128)(2,1)} all-to-all(bf16[64,64,256]{2,1,0:T(8,128)(2,1)S(1)} %broadcast_in_dim.2), channel_id=1, replica_groups=mesh['xl'=2,'co'=2,'z'=4,'xh'=2,'y'=4] {'xl','z','xh','y'}, dimensions={0} | all-to-all | bytes 4194304 | tf_op jit(solution)/shard_map/all_to_all | solution.py:273
  41.4 0.0 copy-start.7
  41.4 0.0 copy-start.5
  41.4 2.1 %collective-permute-start.3 = (bf16[4096,256]{1,0:T(8,128)(2,1)}, bf16[4096,256]{1,0:T(8,128)(2,1)}, u32[]{:S(2)}, u32[]{:S(2)}) collective-permute-start(bf16[4096,256]{1,0:T(8,128)(2,1)} %bitcast.5.mine), channel_id=1, source_target_pairs={{0,32},{32,0},{1,33},{33,1},{2,34},{34,2},{3,35},{35,3},{4,36},{36... | collective-permute-start | bytes 6291464 | tf_op jit(solution)/shard_map/ppermute | solution.py:243
  43.5 0.0 copy-done.6
  43.5 0.1 copy.19
  43.7 0.6 compare_reduce_fusion
  44.3 0.7 broadcast_select_fusion
  45.0 0.6 fusion
  45.6 0.0 copy-done.9
  45.6 0.6 and_reduce_fusion
  46.2 0.0 copy-done.8
  46.2 2.0 %dynamic-slice_select_fusion = f32[2,8]{1,0:T(2,128)S(1)} fusion(s32[]{:T(128)} %bitcast.3, s32[]{:T(128)} %bitcast.4, s32[2,8]{1,0:T(2,128)S(1)} %copy-done.8, pred[]{:T(512)} %and_reduce_fusion, f32[256,4]{1,0:T(8,128)S(1)} %broadcast_select_fusion), kind=kLoop, calls=%fused_computation.5 | loop fusion | flops 32 | bytes 4233 | tf_op jit(solution)/shard_map/select.3
  48.2 1.8 %scatter.9 = f32[256,128]{1,0:T(8,128)S(1)} dynamic-update-slice(f32[256,128]{1,0:T(8,128)S(1)} %scatter.6, f32[2,8]{1,0:T(2,128)S(1)} %dynamic-slice_select_fusion, s32[]{:T(128)} %bitcast.3, s32[]{:T(128)} %bitcast.4) | dynamic-update-slice | bytes 132 | tf_op jit(solution)/shard_map/scatter | solution.py:268
  50.1 0.0 copy-done.3
  50.1 0.0 copy-done.4
  50.1 0.1 collective-permute-start.2
  50.2 1.3 collective-permute-start.1
  51.6 0.8 collective-permute-start
  52.4 0.1 slice.64
  52.4 0.0 copy-done.7
  52.4 0.1 reshape.96
  52.5 0.1 reshape.99
  52.6 0.0 copy-done.5
  52.6 0.2 copy.20.table
  52.9 14.3 %collective-permute-done.2.d3 = f32[256,640]{1,0:T(8,128)S(1)} collective-permute-done((f32[256,640]{1,0:T(8,128)S(1)}, f32[256,640]{1,0:T(8,128)S(1)}, u32[]{:S(2)}, u32[]{:S(2)}) %collective-permute-start.2) | collective-permute-done | bytes 655392 | tf_op jit(solution)/shard_map/ppermute | solution.py:243
  67.2 0.1 slice.67
  67.3 0.1 reshape.102
  67.4 12.9 %collective-permute-done.1.d2 = f32[256,640]{1,0:T(8,128)S(1)} collective-permute-done((f32[256,640]{1,0:T(8,128)S(1)}, f32[256,640]{1,0:T(8,128)S(1)}, u32[]{:S(2)}, u32[]{:S(2)}) %collective-permute-start.1) | collective-permute-done | bytes 655392 | tf_op jit(solution)/shard_map/ppermute | solution.py:243
  80.3 0.1 slice.66
  80.4 0.1 reshape.101
  80.4 0.0 collective-permute-done.d1
  80.5 0.1 slice.65
  80.5 0.1 reshape.100
  80.6 0.1 maximum_convert_fusion
  80.7 0.1 concatenate.15.meta
  80.8 0.0 collective-permute-done.3.other
  80.8 34.1 %shard_map.144 = (f32[256,256]{1,0:T(8,128)}, f32[256,256]{1,0:T(8,128)}, f32[256,4]{1,0:T(8,128)S(1)}, bf16[32,80,256]{2,1,0:T(8,128)(2,1)S(1)}) custom-call(s32[83]{0:T(128)S(1)} %concatenate.15.meta, bf16[4096,256]{1,0:T(8,128)(2,1)} %bitcast.5.mine, bf16[4096,256]{1,0:T(8,128)(2,1)} %collective-permute-done.3.other, f32[256,640]{1,0:T(8,128)S(1)} %pad_maximum_fusion.d0, ...), custom_call_target="tpu_custom_call" | custom-call | tf_op jit(solution)/shard_map/pallas_call | solution.py:282
  114.8 0.0 copy-start
  114.8 0.0 copy-start.1
  114.8 0.0 copy-start.2
  114.9 27.4 %all_to_all.22.got = bf16[32,80,256]{2,1,0:T(8,128)(2,1)S(1)} all-to-all(bf16[32,80,256]{2,1,0:T(8,128)(2,1)S(1)} %get-tuple-element.45), channel_id=1, replica_groups=mesh['xl'=2,'co'=2,'z'=4,'xh'=2,'y'=4] {'z','xh','y'}, dimensions={0} | all-to-all | bytes 2621440 | tf_op jit(solution)/shard_map/all_to_all | solution.py:308
  142.2 2.8 %shard_map.145 = (f32[64,256]{1,0:T(8,128)S(1)}, f32[128,128]{1,0:T(8,128)}, f32[32,1408]{1,0:T(8,128)S(1)}) custom-call(bf16[32,80,256]{2,1,0:T(8,128)(2,1)S(1)} %all_to_all.22.got), custom_call_target="tpu_custom_call" | custom-call | tf_op jit(solution)/shard_map/pallas_call | solution.py:309
  145.0 2.8 %collective-permute-start.6 = (f32[32,1408]{1,0:T(8,128)S(1)}, f32[32,1408]{1,0:T(8,128)S(1)}, u32[]{:S(2)}, u32[]{:S(2)}) collective-permute-start(f32[32,1408]{1,0:T(8,128)S(1)} %get-tuple-element.48.r0), channel_id=1, source_target_pairs={{0,96},{32,64},{64,32},{96,0},{1,97},{33,65},{65,33},{97,1},{2,98}... | collective-permute-start | bytes 540680 | tf_op jit(solution)/shard_map/ppermute | solution.py:243
  147.8 1.2 collective-permute-start.5
  148.9 0.0 collective-permute-start.4
  148.9 3.9 %all-to-all-start.2 = ((f32[128,1,128]{2,1,0:T(1,128)}), f32[128,1,128]{2,1,0:T(1,128)S(1)}, u32[]{:S(2)}, u32[]{:S(2)}) async-start(f32[128,1,128]{2,1,0:T(1,128)} %bitcast.7), calls=%async_computation.2 | async-start | bytes 131072 | tf_op jit(solution)/shard_map/all_to_all | solution.py:321
  152.8 0.7 copy.22
  153.5 9.1 %all-to-all-done.2 = f32[128,1,128]{2,1,0:T(1,128)S(1)} async-done(((f32[128,1,128]{2,1,0:T(1,128)}), f32[128,1,128]{2,1,0:T(1,128)S(1)}, u32[]{:S(2)}, u32[]{:S(2)}) %all-to-all-start.2) | async-done | bytes 65568 | tf_op jit(solution)/shard_map/all_to_all | solution.py:321
  162.6 0.0 collective-permute-done.6.r3
  162.6 0.0 collective-permute-done.5.r2
  162.7 0.0 collective-permute-done.4.r1
  162.7 0.0 copy-done
  162.7 0.0 copy-done.1
  162.7 0.0 copy-done.2
  162.7 0.8 shard_map.146
  163.5 0.7 slice_bitcast_fusion
  (4 shorter events, 0.1 us)
Async XLA Ops:
  1.7 41.8 %copy-start.6 = (s32[256,4]{0,1:T(4,128)S(1)}, s32[256,4]{0,1:T(4,128)}, u32[]{:S(2)}) copy-start(s32[256,4]{0,1:T(4,128)} %param.20) | copy-start | bytes 12292
  1.7 43.8 %copy-start.9 = (s32[2]{0:T(128)S(1)}, s32[2]{0:T(128)}, u32[]{:S(2)}) copy-start(s32[2]{0:T(128)} %constant.64.clone.1) | copy-start | bytes 28
  1.8 44.5 %copy-start.8 = (s32[2,8]{1,0:T(2,128)S(1)}, s32[2,8]{1,0:T(2,128)}, u32[]{:S(2)}) copy-start(s32[2,8]{1,0:T(2,128)} %param.19) | copy-start | bytes 196
  1.8 48.3 %copy-start.3 = (f32[256,256]{1,0:T(8,128)S(1)}, f32[256,256]{1,0:T(8,128)}, u32[]{:S(2)}) copy-start(f32[256,256]{1,0:T(8,128)} %param.14) | copy-start | bytes 786436
  1.8 48.3 %copy-start.4 = (f32[256,256]{1,0:T(8,128)S(1)}, f32[256,256]{1,0:T(8,128)}, u32[]{:S(2)}) copy-start(f32[256,256]{1,0:T(8,128)} %param.13) | copy-start | bytes 786436
  41.4 11.0 %copy-start.7 = (s32[1,4,4]{2,1,0:T(4,128)S(1)}, s32[1,4,4]{2,1,0:T(4,128)}, u32[]{:S(2)}) copy-start(s32[1,4,4]{2,1,0:T(4,128)} %param.21) | copy-start | bytes 196
  41.4 11.2 %copy-start.5 = (f32[1315,32]{0,1:T(8,128)S(1)}, f32[1315,32]{0,1:T(8,128)}, u32[]{:S(2)}) copy-start(f32[1315,32]{0,1:T(8,128)} %param.18) | copy-start | bytes 504964
  41.4 39.4 %collective-permute-start.3 = (bf16[4096,256]{1,0:T(8,128)(2,1)}, bf16[4096,256]{1,0:T(8,128)(2,1)}, u32[]{:S(2)}, u32[]{:S(2)}) collective-permute-start(bf16[4096,256]{1,0:T(8,128)(2,1)} %bitcast.5.mine), channel_id=1, source_target_pairs={{0,32},{32,0},{1,33},{33,1},{2,34},{34,2},{3,35},{35,3},{4,36},{36... | collective-permute-start | bytes 6291464 | tf_op jit(solution)/shard_map/ppermute | solution.py:243
  50.1 17.1 %collective-permute-start.2 = (f32[256,640]{1,0:T(8,128)S(1)}, f32[256,640]{1,0:T(8,128)S(1)}, u32[]{:S(2)}, u32[]{:S(2)}) collective-permute-start(f32[256,640]{1,0:T(8,128)S(1)} %pad_maximum_fusion.d0), channel_id=1, source_target_pairs={{0,96},{32,64},{64,32},{96,0},{1,97},{33,65},{65,33},{97,1},{2,98}... | collective-permute-start | bytes 1966088 | tf_op jit(solution)/shard_map/ppermute | solution.py:243
  50.2 30.0 %collective-permute-start.1 = (f32[256,640]{1,0:T(8,128)S(1)}, f32[256,640]{1,0:T(8,128)S(1)}, u32[]{:S(2)}, u32[]{:S(2)}) collective-permute-start(f32[256,640]{1,0:T(8,128)S(1)} %pad_maximum_fusion.d0), channel_id=1, source_target_pairs={{0,64},{32,96},{64,0},{96,32},{1,65},{33,97},{65,1},{97,33},{2,66}... | collective-permute-start | bytes 1966088 | tf_op jit(solution)/shard_map/ppermute | solution.py:243
  51.6 28.9 %collective-permute-start = (f32[256,640]{1,0:T(8,128)S(1)}, f32[256,640]{1,0:T(8,128)S(1)}, u32[]{:S(2)}, u32[]{:S(2)}) collective-permute-start(f32[256,640]{1,0:T(8,128)S(1)} %pad_maximum_fusion.d0), channel_id=1, source_target_pairs={{0,32},{32,0},{64,96},{96,64},{1,33},{33,1},{65,97},{97,65},{2,34}... | collective-permute-start | bytes 1966088 | tf_op jit(solution)/shard_map/ppermute | solution.py:243
  114.8 47.8 %copy-start = (f32[64,256]{1,0:T(8,128)S(1)}, f32[64,256]{1,0:T(8,128)}, u32[]{:S(2)}) copy-start(f32[64,256]{1,0:T(8,128)} %core.1) | copy-start | bytes 196612
  114.8 47.8 %copy-start.1 = (f32[64,256]{1,0:T(8,128)S(1)}, f32[64,256]{1,0:T(8,128)}, u32[]{:S(2)}) copy-start(f32[64,256]{1,0:T(8,128)} %moment.1) | copy-start | bytes 196612
  114.8 47.8 %copy-start.2 = (f32[64,256]{1,0:T(8,128)S(1)}, f32[64,256]{1,0:T(8,128)}, u32[]{:S(2)}) copy-start(f32[64,256]{1,0:T(8,128)} %second.1) | copy-start | bytes 196612
  145.0 17.7 %collective-permute-start.6 = (f32[32,1408]{1,0:T(8,128)S(1)}, f32[32,1408]{1,0:T(8,128)S(1)}, u32[]{:S(2)}, u32[]{:S(2)}) collective-permute-start(f32[32,1408]{1,0:T(8,128)S(1)} %get-tuple-element.48.r0), channel_id=1, source_target_pairs={{0,96},{32,64},{64,32},{96,0},{1,97},{33,65},{65,33},{97,1},{2,98}... | collective-permute-start | bytes 540680 | tf_op jit(solution)/shard_map/ppermute | solution.py:243
  147.8 14.9 %collective-permute-start.5 = (f32[32,1408]{1,0:T(8,128)S(1)}, f32[32,1408]{1,0:T(8,128)S(1)}, u32[]{:S(2)}, u32[]{:S(2)}) collective-permute-start(f32[32,1408]{1,0:T(8,128)S(1)} %get-tuple-element.48.r0), channel_id=1, source_target_pairs={{0,64},{32,96},{64,0},{96,32},{1,65},{33,97},{65,1},{97,33},{2,66}... | collective-permute-start | bytes 540680 | tf_op jit(solution)/shard_map/ppermute | solution.py:243
  148.9 13.7 %collective-permute-start.4 = (f32[32,1408]{1,0:T(8,128)S(1)}, f32[32,1408]{1,0:T(8,128)S(1)}, u32[]{:S(2)}, u32[]{:S(2)}) collective-permute-start(f32[32,1408]{1,0:T(8,128)S(1)} %get-tuple-element.48.r0), channel_id=1, source_target_pairs={{0,32},{32,0},{64,96},{96,64},{1,33},{33,1},{65,97},{97,65},{2,34}... | collective-permute-start | bytes 540680 | tf_op jit(solution)/shard_map/ppermute | solution.py:243
  148.9 13.7 %all-to-all-start.2 = ((f32[128,1,128]{2,1,0:T(1,128)}), f32[128,1,128]{2,1,0:T(1,128)S(1)}, u32[]{:S(2)}, u32[]{:S(2)}) async-start(f32[128,1,128]{2,1,0:T(1,128)} %bitcast.7), calls=%async_computation.2 | async-start | bytes 131072 | tf_op jit(solution)/shard_map/all_to_all | solution.py:321

commit v2 on v1

v2 whole, which is shorter than its diff:
```python
import jax
import jax.numpy as jnp
from jax import lax
from jax.experimental import pallas as pl
from jax.experimental.pallas import tpu as pltpu
from jax.sharding import Mesh, PartitionSpec as P

DE = 256
DR = 32
TILE = 128
GROUP = 4
PAIR_ROWS = 64
REL_PAD = 1408
WHOLE = 60 * 1024 * 1024

entity_rate = 4.0
core_rate = 0.001
beta_first = 0.2
beta_second = 0.999

AXES = ("xl", "co", "z", "xh", "y")
MEMBERS = ("xl", "co")
GROUPS = ("z", "xh", "y")
CHIPS = ("xl", "z", "xh", "y")

f32 = jnp.float32
bf16 = jnp.bfloat16


def mm(a, b):
    return jnp.dot(a, b, preferred_element_type=f32)


def mm_nt(a, b):
    return lax.dot_general(a, b, (((1,), (1,)), ((), ())), preferred_element_type=f32)


def mm_tn(a, b):
    return lax.dot_general(a, b, (((0,), (0,)), ((), ())), preferred_element_type=f32)


def prepare_kernel(
    heads, tails, positive, tiles, core, out_own, out_core, hits, names, rows, wide, sems
):
    moves = [
        pltpu.make_async_copy(core, rows, sems.at[0]),
        pltpu.make_async_copy(tiles, names, sems.at[1]),
        pltpu.make_async_copy(positive, hits, sems.at[2]),
        pltpu.make_async_copy(heads, out_own.at[0:256, :], sems.at[3]),
        pltpu.make_async_copy(tails, out_own.at[256:512, :], sems.at[4]),
    ]
    for move in moves:
        move.start()
    moves[0].wait()
    low = rows[...].astype(bf16)
    for d in range(64):
        wide[d] = low
    spread_out = pltpu.make_async_copy(wide, out_core, sems.at[5])
    spread_out.start()
    pick = lax.broadcasted_iota(jnp.int32, (8, 8), 0) == lax.broadcasted_iota(
        jnp.int32, (8, 8), 1
    )
    out_own[512:544, :] = jnp.zeros((32, 256), f32)
    moves[1].wait()
    moves[2].wait()
    ids = names[...].astype(f32)
    out_own[512 : 512 + GROUP, :] = hits[...].astype(f32)
    for i in range(2):
        out_own[528 + 8 * i : 536 + 8 * i, 0:1] = jnp.sum(
            jnp.where(pick, ids[i : i + 1, :], 0.0), axis=1, keepdims=True
        )
    moves[3].wait()
    moves[4].wait()
    spread_out.wait()


def train_kernel(
    meta,
    mine,
    other,
    d0,
    d1,
    d2,
    d3,
    table,
    out_head,
    out_tail,
    out_loss,
    out_pay,
    table_low,
    spread,
    spread_t,
    cores,
    grads,
    heads,
    heads_low,
    heads_part,
    tails,
    tails_low,
    rel_core,
    grad_relcore,
    slopes,
    mine_here,
    other_here,
    sems,
):
    fetch_mine = pltpu.make_async_copy(mine, mine_here, sems.at[0])
    fetch_other = pltpu.make_async_copy(other, other_here, sems.at[1])
    fetch_mine.start()
    fetch_other.start()
    member = meta[0]
    co = meta[1]
    xl = meta[2]
    given = (d0, d1, d2, d3)
    rel_count = table.shape[1]

    table_low[...] = jnp.zeros_like(table_low)
    table_low[:, 0:rel_count] = table[...].astype(bf16)
    ids = jnp.concatenate([d[528:544, 0:1] for d in given], axis=0)
    hot = (
        ids == lax.broadcasted_iota(jnp.int32, (PAIR_ROWS, REL_PAD), 1).astype(f32)
    ).astype(f32).astype(bf16)
    rel_low = mm_nt(hot, table_low[...]).astype(bf16)
    copies = (
        lax.broadcasted_iota(jnp.int32, (DR, 256), 1) % DR
        == lax.broadcasted_iota(jnp.int32, (DR, 256), 0)
    ).astype(f32).astype(bf16)
    rel_wide = mm(rel_low, copies)
    on_row = (
        lax.broadcasted_iota(jnp.int32, (64, 8, 256), 2) // DR
        == lax.broadcasted_iota(jnp.int32, (64, 8, 256), 1)
    )
    spread_f = jnp.where(on_row, rel_wide[:, None, :], 0.0).reshape(512, 256)
    spread[...] = spread_f.astype(bf16)
    spread_t[...] = spread_f.T.astype(bf16)

    def core_step(src, side, q):
        row = pl.multiple_of(q * 512, 512)
        parts = [
            mm(spread[...], src[pl.ds(row + 256 * e, 256), :]).reshape(64, 8, 256)
            for e in range(2)
        ]
        at = 64 * (2 * (q // 4) + side) + 16 * (q % 4)
        cores[:, pl.ds(pl.multiple_of(at, 16), 16), :] = jnp.concatenate(parts, axis=1).astype(bf16)

    for fetch, src, side in ((fetch_mine, mine_here, co), (fetch_other, other_here, 1 - co)):
        fetch.wait()

        @pl.loop(0, 8, unroll=4)
        def _(q, src=src, side=side):
            core_step(src, side, q)

    for s in range(GROUP):
        heads[s] = given[s][0:256, :]
        tails[s] = given[s][256:512, :]

    row = lax.broadcasted_iota(jnp.int32, (TILE, 256), 0)
    half = pl.multiple_of((member // 2) * 128, 128)
    odd = member % 2 == 1

    def round_step(k, last):
        parts = [meta[3 + k * GROUP + (member ^ s)] for s in range(GROUP)]
        slots = range(GROUP)
        for s in slots:
            tails_low[s] = tails[parts[s] ^ member].astype(bf16)
            heads_low[s] = heads[s].astype(bf16)
            heads_part[s] = heads[s, :, pl.ds(half, 128)].T.astype(bf16)

        def at(s, i, j):
            return ((s * 2 + i) * GROUP + parts[s]) * 2 + j

        for s in slots:
            for i in range(2):
                rows = slice(TILE * i, TILE * i + TILE)
                for j in range(2):
                    rel_core[s, j, rows, :] = mm(heads_low[s, rows, :], cores[at(s, i, j)]).astype(
                        bf16
                    )
        for s in slots:
            positive = given[s][pl.ds(512 + parts[s], 1), :].astype(jnp.int32)
            row_loss = None
            for j in range(2):
                score = mm_nt(tails_low[s, TILE * j : TILE * j + TILE, :], rel_core[s, j])
                hit = row + TILE * j == positive
                signed = jnp.where(hit, -score, score)
                slopes[s, j] = (
                    jax.nn.sigmoid(signed) * jnp.where(hit, -1.0, 1.0 / 256.0)
                ).astype(bf16)
                if s == 0:
                    part = jnp.sum(
                        (jnp.maximum(signed, 0.0) + jnp.log1p(jnp.exp(-jnp.abs(signed))))
                        * jnp.where(hit, 1.0, 1.0 / 256.0),
                        axis=0,
                        keepdims=True,
                    )
                    row_loss = part if row_loss is None else row_loss + part
            if s == 0:
                line = lax.broadcasted_iota(jnp.int32, (GROUP, 256), 0) == k
                out_loss[...] = jnp.where(line, row_loss, out_loss[...])
        for s in slots:
            for j in range(2):
                cols = slice(TILE * j, TILE * j + TILE)
                grad_relcore[s, j] = mm_tn(slopes[s, j], tails_low[s, cols, :]).astype(bf16)
        for s in slots:
            for i in range(2):
                rows = slice(TILE * i, TILE * i + TILE)
                for j in range(2):
                    outer = mm(heads_part[s, :, rows], grad_relcore[s, j, rows, :])
                    grads[at(s, i, j)] = jnp.where(odd, outer[64:], outer[:64])
        for s in slots[:1] if last else slots:
            for i in range(2):
                rows = slice(TILE * i, TILE * i + TILE)
                grad_head = mm_nt(grad_relcore[s, 0, rows, :], cores[at(s, i, 0)])
                grad_head = grad_head + mm_nt(grad_relcore[s, 1, rows, :], cores[at(s, i, 1)])
                heads[s, rows, :] -= entity_rate * grad_head
        for s in slots:
            for j in range(2):
                cols = slice(TILE * j, TILE * j + TILE)
                tails[parts[s] ^ member, cols, :] -= entity_rate * mm(slopes[s, j], rel_core[s, j])

    out_loss[...] = jnp.zeros_like(out_loss)

    @pl.loop(0, GROUP - 1)
    def _(k):
        round_step(k, False)

    round_step(GROUP - 1, True)
    out_head[...] = heads[0]
    out_tail[...] = tails[0]

    total = jnp.zeros((512, 256), f32)
    for e in range(8):
        low = grads[:, 8 * e : 8 * e + 8, :].reshape(512, 256).astype(bf16)
        part = mm(spread_t[...], low).astype(bf16)
        for d in range(4):
            out_pay[4 * e + d, 0:64, :] = part[64 * d : 64 * d + 64, :]
        own_core = mine_here[pl.ds(pl.multiple_of(xl * 2048 + 256 * e, 256), 256), :]
        total = total + mm_nt(low, own_core)
    wide = jnp.sum(jnp.where(on_row, total.reshape(64, 8, 256), 0.0), axis=1)
    folded = wide[:, :128] + wide[:, 128:]
    folded = folded + pltpu.roll(folded, 64, 1)
    folded = folded + pltpu.roll(folded, 32, 1)
    lanes = lax.broadcasted_iota(jnp.int32, (16, 128), 1)
    packed = jnp.zeros((16, 128), f32)
    names = jnp.zeros((16, 128), f32)
    for q in range(4):
        own_ids = given[q][528:544, 0:1]
        high = jnp.floor(own_ids * (1.0 / 256.0))
        rest = own_ids - 256.0 * high
        packed = jnp.where(lanes // 32 == q, folded[16 * q : 16 * q + 16, :], packed)
        names = jnp.where(lanes == 32 * q, high, jnp.where(lanes == 32 * q + 1, rest, names))
    tag = jnp.concatenate([packed, names], axis=1).astype(bf16)
    for d in range(32):
        out_pay[d, 64:80, :] = tag


def sum_kernel(got, out_grad, out_square, out_rel):
    total = got[0, 0:64, :].astype(f32)
    for d in range(1, 32):
        total = total + got[d, 0:64, :].astype(f32)
    out_grad[...] = total
    out_square[...] = jnp.full((128, 128), jnp.sum(total * total))
    tags = got[:, 64:80, :].reshape(512, 256)
    values = tags[:, :128].astype(f32).T.astype(bf16)
    names = tags[:, 128:].astype(f32)
    for e in range(REL_PAD // 128):
        lane = (lax.broadcasted_iota(jnp.int32, (512, 128), 1) + 128 * e).astype(f32)
        out = jnp.zeros((DR, 128), f32)
        for q in range(4):
            rid = names[:, 32 * q : 32 * q + 1] * 256.0 + names[:, 32 * q + 1 : 32 * q + 2]
            hot = (lane == rid).astype(f32).astype(bf16)
            out = out + mm(values[32 * q : 32 * q + 32, :], hot)
        out_rel[:, 128 * e : 128 * e + 128] = out


def adam_kernel(
    squares, own, core, moment, second, r0, r1, r2, r3, out_core, out_moment, out_second, out_rel
):
    mean_square = jnp.sum(squares[...]) * (1.0 / 128.0 / (DE * DR * DE))
    scale = jnp.full((1, 1), mean_square) + 1e-06
    normalized = own[...] / jnp.sqrt(scale)
    moment_updated = beta_first * moment[...] + (1.0 - beta_first) * normalized
    second_updated = beta_second * second[...] + (1.0 - beta_second) * normalized * normalized
    out_moment[...] = moment_updated
    out_second[...] = second_updated
    out_core[...] = core[...] - core_rate * moment_updated / (jnp.sqrt(second_updated) + 1e-08)
    total = (r0[...] + r1[...]) + (r2[...] + r3[...])
    out_rel[...] = total[:, : out_rel.shape[1]]


def exchange(value, axes, step):
    size = lax.axis_size(axes)
    return lax.ppermute(value, axes, [(i, i ^ step) for i in range(size)])


def vmem(count):
    return [pl.BlockSpec(memory_space=pltpu.VMEM)] * count


def body(
    head_vectors,
    tail_vectors,
    core_tensor,
    core_moment,
    core_second,
    relation_table,
    tile_relation,
    positive_tail,
    partner_table,
):
    member = lax.axis_index(MEMBERS)
    co = lax.axis_index("co")
    xl = lax.axis_index("xl")
    rel_count = relation_table.shape[0]

    own, low = pl.pallas_call(
        prepare_kernel,
        out_shape=(
            jax.ShapeDtypeStruct((544, DE), f32),
            jax.ShapeDtypeStruct((64, 64, DE), bf16),
        ),
        in_specs=[pl.BlockSpec(memory_space=pl.ANY)] * 5,
        out_specs=(pl.BlockSpec(memory_space=pltpu.VMEM), pl.BlockSpec(memory_space=pl.ANY)),
        scratch_shapes=[
            pltpu.VMEM((GROUP, 256), jnp.int32),
            pltpu.VMEM((2, 8), jnp.int32),
            pltpu.VMEM((64, DE), f32),
            pltpu.VMEM((64, 64, DE), bf16),
            pltpu.SemaphoreType.DMA((6,)),
        ],
        compiler_params=pltpu.CompilerParams(vmem_limit_bytes=WHOLE),
    )(head_vectors, tail_vectors, positive_tail.T, tile_relation, core_tensor)
    across = exchange(own, "xl", 1)
    beside = exchange(own, "co", 1)

    mine = lax.all_to_all(low, CHIPS, split_axis=0, concat_axis=0, tiled=True).reshape(4096, DE)
    mine, across = lax.optimization_barrier((mine, across))
    other = exchange(mine, "co", 1)
    group = [own, beside, across, exchange(across, "co", 1)]

    meta = jnp.concatenate(
        [jnp.stack([member, co, xl]).astype(jnp.int32), partner_table.reshape(-1)]
    )
    head_now, tail_now, loss_now, pay = pl.pallas_call(
        train_kernel,
        out_shape=(
            jax.ShapeDtypeStruct((256, DE), f32),
            jax.ShapeDtypeStruct((256, DE), f32),
            jax.ShapeDtypeStruct((GROUP, 256), f32),
            jax.ShapeDtypeStruct((32, 80, DE), bf16),
        ),
        in_specs=[pl.BlockSpec(memory_space=pltpu.SMEM)]
        + [pl.BlockSpec(memory_space=pl.ANY)] * 2
        + vmem(5),
        out_specs=tuple(vmem(4)),
        scratch_shapes=[
            pltpu.VMEM((DR, REL_PAD), bf16),
            pltpu.VMEM((512, 256), bf16),
            pltpu.VMEM((256, 512), bf16),
            pltpu.VMEM((64, 256, 256), bf16),
            pltpu.VMEM((64, 64, 256), f32),
            pltpu.VMEM((GROUP, 256, DE), f32),
            pltpu.VMEM((GROUP, 256, DE), bf16),
            pltpu.VMEM((GROUP, 128, DE), bf16),
            pltpu.VMEM((GROUP, 256, DE), f32),
            pltpu.VMEM((GROUP, 256, DE), bf16),
            pltpu.VMEM((GROUP, 2, 256, DE), bf16),
            pltpu.VMEM((GROUP, 2, 256, DE), bf16),
            pltpu.VMEM((GROUP, 2, TILE, DE), bf16),
            pltpu.VMEM((4096, DE), bf16),
            pltpu.VMEM((4096, DE), bf16),
            pltpu.SemaphoreType.DMA((2,)),
        ],
        compiler_params=pltpu.CompilerParams(vmem_limit_bytes=48 * 1024 * 1024),
    )(meta, mine, other, *group, relation_table.T)

    got = lax.all_to_all(pay, GROUPS, split_axis=0, concat_axis=0, tiled=True)
    own_grad, square, rel_part = pl.pallas_call(
        sum_kernel,
        out_shape=(
            jax.ShapeDtypeStruct((64, DE), f32),
            jax.ShapeDtypeStruct((128, 128), f32),
            jax.ShapeDtypeStruct((DR, REL_PAD), f32),
        ),
        in_specs=vmem(1),
        out_specs=tuple(vmem(3)),
        compiler_params=pltpu.CompilerParams(vmem_limit_bytes=32 * 1024 * 1024),
    )(got)
    rel_parts = [rel_part] + [exchange(rel_part, MEMBERS, s) for s in range(1, GROUP)]
    squares = lax.all_to_all(square, AXES, split_axis=0, concat_axis=0, tiled=True)
    core_updated, moment_updated, second_updated, rel_sum = pl.pallas_call(
        adam_kernel,
        out_shape=(
            jax.ShapeDtypeStruct((64, DE), f32),
            jax.ShapeDtypeStruct((64, DE), f32),
            jax.ShapeDtypeStruct((64, DE), f32),
            jax.ShapeDtypeStruct((DR, rel_count), f32),
        ),
        in_specs=vmem(9),
        out_specs=tuple(vmem(4)),
        compiler_params=pltpu.CompilerParams(vmem_limit_bytes=32 * 1024 * 1024),
    )(squares, own_grad, core_tensor, core_moment, core_second, *rel_parts)
    return (
        head_now,
        tail_now,
        loss_now.T,
        core_updated,
        moment_updated,
        second_updated,
        rel_sum.T,
    )


def solution(mesh):
    fine = Mesh(mesh.devices.reshape(2, 2, 4, 2, 4), AXES)
    rows = P(AXES, None)
    return jax.shard_map(
        body,
        mesh=fine,
        in_specs=(rows, rows, rows, rows, rows, P(), rows, rows, P(GROUPS, None, None)),
        out_specs=(rows, rows, rows, rows, rows, rows, P()),
        check_vma=False,
    )
```

time: 165 us -> 124 us (0.75)
  blocking collectives: 67 us -> 42.8 us
  Pallas kernels: 37.7 us -> 21.9 us
  starting transfers between devices: 12.1 us -> 19.5 us
  local copies, waits for them, and re-layouts: 5.24 us -> 0.12 us
  other arithmetic: 4.94 us -> 0.08 us
  waiting for transfers between devices: 36.4 us -> 38.8 us
    all_to_all x1, blocking collectives: 39.6 us -> 13.3 us  [body(): lax.all_to_all(square, AXES, split_axis=0, concat_axis=0, tiled=True)]
    pallas_call x1, Pallas kernels: 34.1 us -> 16.3 us  [body(): pl.pallas_call(train_kernel, out_shape=(jax.ShapeDtypeStruct((256, DE), f...]
    ppermute x7, waiting for transfers between devices: 27.3 us -> 38.8 us  [exchange(): return lax.ppermute(value, axes, [(i, i ^ step) for i in range(size)])]
    all_to_all x1, waiting for transfers between devices: 9.13 us -> 0.01 us  [body(): lax.all_to_all(low, CHIPS, split_axis=0, concat_axis=0, tiled=True)]
    all_to_all x1, starting transfers between devices: 3.89 us -> 12.1 us  [body(): lax.all_to_all(low, CHIPS, split_axis=0, concat_axis=0, tiled=True)]
    another operation x5 -> x0, other arithmetic: 3.96 us -> none
    pallas_call x0 -> x1, Pallas kernels: none -> 3.29 us  [body(): pl.pallas_call(prepare_kernel, out_shape=(jax.ShapeDtypeStruct((544, DE),...]
    all_to_all x1, blocking collectives: 27.4 us -> 29.6 us  [body(): got = lax.all_to_all(pay, GROUPS, split_axis=0, concat_axis=0, tiled=True)]
  transfers between devices with their start and end apart: 8 -> 8, of which waited for: 3 -> 3; matrix products, arithmetic and copies ran while one was open for 5% -> 0% of each run, Pallas kernels for 0% -> 0%
where the time goes in v2:
time: 124 us
  blocking collectives  42.8 us (35%)
  waiting for transfers between devices  38.8 us (31%)
  Pallas kernels  21.9 us (18%)
  starting transfers between devices  19.5 us (16%)
    ppermute x7, waiting for transfers between devices, exchange(): return lax.ppermute(value, axes, [(i, i ^ step) for i in range(size)])  38.8 us
    all_to_all x1, blocking collectives, body(): got = lax.all_to_all(pay, GROUPS, split_axis=0, concat_axis=0, tiled=True)  29.6 us
    pallas_call x1, Pallas kernels, body(): pl.pallas_call(train_kernel, out_shape=(jax.ShapeDtypeStruct((256, DE), f...  16.3 us
    all_to_all x1, blocking collectives, body(): lax.all_to_all(square, AXES, split_axis=0, concat_axis=0, tiled=True)  13.3 us
    all_to_all x1, starting transfers between devices, body(): lax.all_to_all(low, CHIPS, split_axis=0, concat_axis=0, tiled=True)  12.1 us
    ppermute x7, starting transfers between devices, exchange(): return lax.ppermute(value, axes, [(i, i ^ step) for i in range(size)])  7.36 us
    pallas_call x1, Pallas kernels, body(): pl.pallas_call(prepare_kernel, out_shape=(jax.ShapeDtypeStruct((544, DE),...  3.29 us
  transfers between devices with their start and end apart: 8, of which 3 were waited for; matrix products, arithmetic and copies ran while one was open for 0% of the time, Pallas kernels for 0%

profile of v2, /device:TPU:1, one launch (start us, length us, event | category | flops | bytes accessed | tf_op | source)
XLA Modules:
  0.0 123.9 jit_solution(14165382548408058566)
XLA Ops:
  0.6 3.3 %shard_map.144 = (f32[544,256]{1,0:T(8,128)}, bf16[64,64,256]{2,1,0:T(8,128)(2,1)}) custom-call(f32[256,256]{1,0:T(8,128)} %heads.1, f32[256,256]{1,0:T(8,128)} %tails.1, s32[4,256]{1,0:T(4,128)} %bitcast.17, s32[2,8]{1,0:T(2,128)} %tiles.1, f32[64,256]{1,0:T(8,128)} %core.3), custom_call_target="tpu_custom_call" | custom-call | tf_op jit(solution)/shard_map/pallas_call | solution.py:316
  3.9 0.0 copy-start
  3.9 0.0 copy-start.5
  4.0 0.0 copy-start.2
  4.0 12.1 %all-to-all-start = ((bf16[64,64,256]{2,1,0:T(8,128)(2,1)}), bf16[64,64,256]{2,1,0:T(8,128)(2,1)S(1)}, u32[]{:S(2)}, u32[]{:S(2)}) async-start(bf16[64,64,256]{2,1,0:T(8,128)(2,1)} %get-tuple-element.22), calls=%async_computation | async-start | bytes 4194304 | tf_op jit(solution)/shard_map/all_to_all | solution.py:336
  16.1 0.0 copy-done
  16.1 1.2 collective-permute-start
  17.3 33.9 %collective-permute-done.d2 = f32[544,256]{1,0:T(8,128)S(1)} collective-permute-done((f32[544,256]{1,0:T(8,128)S(1)}, f32[544,256]{1,0:T(8,128)S(1)}, u32[]{:S(2)}, u32[]{:S(2)}) %collective-permute-start) | collective-permute-done | bytes 557088 | tf_op jit(solution)/shard_map/ppermute | solution.py:293
  51.2 0.0 all-to-all-done
  51.2 1.9 %collective-permute-start.1 = (bf16[4096,256]{1,0:T(8,128)(2,1)S(1)}, bf16[4096,256]{1,0:T(8,128)(2,1)}, u32[]{:S(2)}, u32[]{:S(2)}) collective-permute-start(bf16[4096,256]{1,0:T(8,128)(2,1)S(1)} %bitcast.12), channel_id=1, source_target_pairs={{0,32},{32,0},{1,33},{33,1},{2,34},{34,2},{3,35},{35,3},{4,36},{36... | collective-permute-start | bytes 6291464 | tf_op jit(solution)/shard_map/ppermute | solution.py:293
  53.1 0.0 collective-permute-start.2
  53.1 0.5 collective-permute-start.3
  53.6 0.0 copy-done.5
  53.6 0.1 reshape.22
  53.7 0.1 pad_add_fusion.meta
  53.8 4.0 %collective-permute-done.2.d1 = f32[544,256]{1,0:T(8,128)} collective-permute-done((f32[544,256]{1,0:T(8,128)S(1)}, f32[544,256]{1,0:T(8,128)}, u32[]{:S(2)}, u32[]{:S(2)}) %collective-permute-start.2) | collective-permute-done | bytes 557088 | tf_op jit(solution)/shard_map/ppermute | solution.py:293
  57.8 0.8 collective-permute-done.3.d3
  58.6 0.0 collective-permute-done.1.other
  58.6 0.0 copy-done.2
  58.6 16.3 %shard_map.145 = (f32[256,256]{1,0:T(8,128)}, f32[256,256]{1,0:T(8,128)}, f32[4,256]{1,0:T(4,128)}, bf16[32,80,256]{2,1,0:T(8,128)(2,1)S(1)}) custom-call(s32[19]{0:T(128)S(1)} %pad_add_fusion.meta, bf16[4096,256]{1,0:T(8,128)(2,1)S(1)} %bitcast.13, bf16[4096,256]{1,0:T(8,128)(2,1)} %collective-permute-done.1.other, f32[544,256]{1,0:T(8,128)S(1)} %copy-done, ...), custom_call_target="tpu_custom_call" | custom-call | tf_op jit(solution)/shard_map/pallas_call | solution.py:344
  74.9 0.0 copy-start.1
  74.9 0.0 copy-start.3
  74.9 0.0 copy-start.4
  74.9 29.6 %all_to_all.21.got = bf16[32,80,256]{2,1,0:T(8,128)(2,1)S(1)} all-to-all(bf16[32,80,256]{2,1,0:T(8,128)(2,1)S(1)} %get-tuple-element.29), channel_id=1, replica_groups=mesh['xl'=2,'co'=2,'z'=4,'xh'=2,'y'=4] {'z','xh','y'}, dimensions={0} | all-to-all | bytes 2621440 | tf_op jit(solution)/shard_map/all_to_all | solution.py:377
  104.5 1.5 %shard_map.146 = (f32[64,256]{1,0:T(8,128)S(1)}, f32[128,128]{1,0:T(8,128)S(1)}, f32[32,1408]{1,0:T(8,128)S(1)}) custom-call(bf16[32,80,256]{2,1,0:T(8,128)(2,1)S(1)} %all_to_all.21.got), custom_call_target="tpu_custom_call" | custom-call | tf_op jit(solution)/shard_map/pallas_call | solution.py:378
  105.9 2.1 %collective-permute-start.6 = (f32[32,1408]{1,0:T(8,128)S(1)}, f32[32,1408]{1,0:T(8,128)S(1)}, u32[]{:S(2)}, u32[]{:S(2)}) collective-permute-start(f32[32,1408]{1,0:T(8,128)S(1)} %get-tuple-element.32.r0), channel_id=1, source_target_pairs={{0,96},{32,64},{64,32},{96,0},{1,97},{33,65},{65,33},{97,1},{2,98}... | collective-permute-start | bytes 540680 | tf_op jit(solution)/shard_map/ppermute | solution.py:293
  108.0 1.7 %collective-permute-start.5 = (f32[32,1408]{1,0:T(8,128)S(1)}, f32[32,1408]{1,0:T(8,128)S(1)}, u32[]{:S(2)}, u32[]{:S(2)}) collective-permute-start(f32[32,1408]{1,0:T(8,128)S(1)} %get-tuple-element.32.r0), channel_id=1, source_target_pairs={{0,64},{32,96},{64,0},{96,32},{1,65},{33,97},{65,1},{97,33},{2,66}... | collective-permute-start | bytes 540680 | tf_op jit(solution)/shard_map/ppermute | solution.py:293
  109.7 0.0 collective-permute-start.4
  109.7 13.3 %all_to_all.22 = f32[128,1,128]{2,1,0:T(1,128)S(1)} all-to-all(f32[128,1,128]{2,1,0:T(1,128)S(1)} %bitcast.16), channel_id=1, replica_groups=mesh['xl'=2,'co'=2,'z'=4,'xh'=2,'y'=4] {'xl','co','z','xh','y'}, dimensions={0} | all-to-all | bytes 131072 | tf_op jit(solution)/shard_map/all_to_all | solution.py:390
  123.0 0.0 collective-permute-done.6.r3
  123.0 0.0 collective-permute-done.5.r2
  123.0 0.0 collective-permute-done.4.r1
  123.0 0.0 copy-done.1
  123.0 0.0 copy-done.3
  123.0 0.0 copy-done.4
  123.0 0.9 shard_map.147
Async XLA Ops:
  3.9 12.2 %copy-start = (f32[544,256]{1,0:T(8,128)S(1)}, f32[544,256]{1,0:T(8,128)}, u32[]{:S(2)}) copy-start(f32[544,256]{1,0:T(8,128)} %get-tuple-element.23.d0) | copy-start | bytes 1671172
  3.9 49.7 %copy-start.5 = (s32[1,4,4]{2,1,0:T(4,128)S(1)}, s32[1,4,4]{2,1,0:T(4,128)}, u32[]{:S(2)}) copy-start(s32[1,4,4]{2,1,0:T(4,128)} %param.17) | copy-start | bytes 196
  4.0 54.6 %copy-start.2 = (f32[1315,32]{0,1:T(8,128)S(1)}, f32[1315,32]{0,1:T(8,128)}, u32[]{:S(2)}) copy-start(f32[1315,32]{0,1:T(8,128)} %param.14) | copy-start | bytes 504964
  4.0 47.2 %all-to-all-start = ((bf16[64,64,256]{2,1,0:T(8,128)(2,1)}), bf16[64,64,256]{2,1,0:T(8,128)(2,1)S(1)}, u32[]{:S(2)}, u32[]{:S(2)}) async-start(bf16[64,64,256]{2,1,0:T(8,128)(2,1)} %get-tuple-element.22), calls=%async_computation | async-start | bytes 4194304 | tf_op jit(solution)/shard_map/all_to_all | solution.py:336
  16.1 35.1 %collective-permute-start = (f32[544,256]{1,0:T(8,128)S(1)}, f32[544,256]{1,0:T(8,128)S(1)}, u32[]{:S(2)}, u32[]{:S(2)}) collective-permute-start(f32[544,256]{1,0:T(8,128)S(1)} %copy-done), channel_id=1, source_target_pairs={{0,64},{64,0},{1,65},{65,1},{2,66},{66,2},{3,67},{67,3},{4,68},{68... | collective-permute-start | bytes 1671176 | tf_op jit(solution)/shard_map/ppermute | solution.py:293
  51.2 7.4 %collective-permute-start.1 = (bf16[4096,256]{1,0:T(8,128)(2,1)S(1)}, bf16[4096,256]{1,0:T(8,128)(2,1)}, u32[]{:S(2)}, u32[]{:S(2)}) collective-permute-start(bf16[4096,256]{1,0:T(8,128)(2,1)S(1)} %bitcast.12), channel_id=1, source_target_pairs={{0,32},{32,0},{1,33},{33,1},{2,34},{34,2},{3,35},{35,3},{4,36},{36... | collective-permute-start | bytes 6291464 | tf_op jit(solution)/shard_map/ppermute | solution.py:293
  53.1 4.7 %collective-permute-start.2 = (f32[544,256]{1,0:T(8,128)S(1)}, f32[544,256]{1,0:T(8,128)}, u32[]{:S(2)}, u32[]{:S(2)}) collective-permute-start(f32[544,256]{1,0:T(8,128)S(1)} %copy-done), channel_id=1, source_target_pairs={{0,32},{32,0},{1,33},{33,1},{2,34},{34,2},{3,35},{35,3},{4,36},{36... | collective-permute-start | bytes 1671176 | tf_op jit(solution)/shard_map/ppermute | solution.py:293
  53.1 5.5 %collective-permute-start.3 = (f32[544,256]{1,0:T(8,128)S(1)}, f32[544,256]{1,0:T(8,128)}, u32[]{:S(2)}, u32[]{:S(2)}) collective-permute-start(f32[544,256]{1,0:T(8,128)S(1)} %collective-permute-done.d2), channel_id=1, source_target_pairs={{0,32},{32,0},{1,33},{33,1},{2,34},{34,2},{3,35},{35,3},{4,36},{36... | collective-permute-start | bytes 1671176 | tf_op jit(solution)/shard_map/ppermute | solution.py:293
  74.9 48.1 %copy-start.1 = (f32[64,256]{1,0:T(8,128)S(1)}, f32[64,256]{1,0:T(8,128)}, u32[]{:S(2)}) copy-start(f32[64,256]{1,0:T(8,128)} %core.3) | copy-start | bytes 196612
  74.9 48.1 %copy-start.3 = (f32[64,256]{1,0:T(8,128)S(1)}, f32[64,256]{1,0:T(8,128)}, u32[]{:S(2)}) copy-start(f32[64,256]{1,0:T(8,128)} %moment.1) | copy-start | bytes 196612
  74.9 48.1 %copy-start.4 = (f32[64,256]{1,0:T(8,128)S(1)}, f32[64,256]{1,0:T(8,128)}, u32[]{:S(2)}) copy-start(f32[64,256]{1,0:T(8,128)} %second.1) | copy-start | bytes 196612
  105.9 17.1 %collective-permute-start.6 = (f32[32,1408]{1,0:T(8,128)S(1)}, f32[32,1408]{1,0:T(8,128)S(1)}, u32[]{:S(2)}, u32[]{:S(2)}) collective-permute-start(f32[32,1408]{1,0:T(8,128)S(1)} %get-tuple-element.32.r0), channel_id=1, source_target_pairs={{0,96},{32,64},{64,32},{96,0},{1,97},{33,65},{65,33},{97,1},{2,98}... | collective-permute-start | bytes 540680 | tf_op jit(solution)/shard_map/ppermute | solution.py:293
  108.0 15.0 %collective-permute-start.5 = (f32[32,1408]{1,0:T(8,128)S(1)}, f32[32,1408]{1,0:T(8,128)S(1)}, u32[]{:S(2)}, u32[]{:S(2)}) collective-permute-start(f32[32,1408]{1,0:T(8,128)S(1)} %get-tuple-element.32.r0), channel_id=1, source_target_pairs={{0,64},{32,96},{64,0},{96,32},{1,65},{33,97},{65,1},{97,33},{2,66}... | collective-permute-start | bytes 540680 | tf_op jit(solution)/shard_map/ppermute | solution.py:293
  109.7 13.3 %collective-permute-start.4 = (f32[32,1408]{1,0:T(8,128)S(1)}, f32[32,1408]{1,0:T(8,128)S(1)}, u32[]{:S(2)}, u32[]{:S(2)}) collective-permute-start(f32[32,1408]{1,0:T(8,128)S(1)} %get-tuple-element.32.r0), channel_id=1, source_target_pairs={{0,32},{32,0},{64,96},{96,64},{1,33},{33,1},{65,97},{97,65},{2,34}... | collective-permute-start | bytes 540680 | tf_op jit(solution)/shard_map/ppermute | solution.py:293

commit v3 on v2

--- a/solution.py
+++ b/solution.py
@@ -40,14 +40,14 @@
 
 
 def prepare_kernel(
-    heads, tails, positive, tiles, core, out_own, out_core, hits, names, rows, wide, sems
+    heads, tails, positive, tiles, core, out_own, out_core, hits, names, rows, both, wide, sems
 ):
     moves = [
         pltpu.make_async_copy(core, rows, sems.at[0]),
-        pltpu.make_async_copy(tiles, names, sems.at[1]),
-        pltpu.make_async_copy(positive, hits, sems.at[2]),
-        pltpu.make_async_copy(heads, out_own.at[0:256, :], sems.at[3]),
-        pltpu.make_async_copy(tails, out_own.at[256:512, :], sems.at[4]),
+        pltpu.make_async_copy(heads, both.at[0:256, :], sems.at[1]),
+        pltpu.make_async_copy(tails, both.at[256:512, :], sems.at[2]),
+        pltpu.make_async_copy(tiles, names, sems.at[3]),
+        pltpu.make_async_copy(positive, hits, sems.at[4]),
     ]
     for move in moves:
         move.start()
@@ -57,20 +57,20 @@
         wide[d] = low
     spread_out = pltpu.make_async_copy(wide, out_core, sems.at[5])
     spread_out.start()
+    for move in moves[1:]:
+        move.wait()
     pick = lax.broadcasted_iota(jnp.int32, (8, 8), 0) == lax.broadcasted_iota(
         jnp.int32, (8, 8), 1
     )
-    out_own[512:544, :] = jnp.zeros((32, 256), f32)
-    moves[1].wait()
-    moves[2].wait()
+    both[512:544, :] = jnp.zeros((32, 256), f32)
+    both[512 : 512 + GROUP, :] = hits[...].astype(f32)
     ids = names[...].astype(f32)
-    out_own[512 : 512 + GROUP, :] = hits[...].astype(f32)
     for i in range(2):
-        out_own[528 + 8 * i : 536 + 8 * i, 0:1] = jnp.sum(
-            jnp.where(pick, ids[i : i + 1, :], 0.0), axis=1, keepdims=True
-        )
-    moves[3].wait()
-    moves[4].wait()
+        column = jnp.sum(jnp.where(pick, ids[i : i + 1, :], 0.0), axis=1, keepdims=True)
+        high = jnp.floor(column * (1.0 / 256.0))
+        both[528 + 8 * i : 536 + 8 * i, 0:1] = high
+        both[528 + 8 * i : 536 + 8 * i, 1:2] = column - 256.0 * high
+    out_own[...] = both[...].astype(bf16)
     spread_out.wait()
 
 
@@ -78,6 +78,8 @@
     meta,
     mine,
     other,
+    own_heads,
+    own_tails,
     d0,
     d1,
     d2,
@@ -110,13 +112,14 @@
     fetch_other.start()
     member = meta[0]
     co = meta[1]
-    xl = meta[2]
+    side = meta[2]
     given = (d0, d1, d2, d3)
     rel_count = table.shape[1]
 
     table_low[...] = jnp.zeros_like(table_low)
     table_low[:, 0:rel_count] = table[...].astype(bf16)
-    ids = jnp.concatenate([d[528:544, 0:1] for d in given], axis=0)
+    names = [d[528:544, 0:128].astype(f32) for d in given]
+    ids = jnp.concatenate([d[:, 0:1] * 256.0 + d[:, 1:2] for d in names], axis=0)
     hot = (
         ids == lax.broadcasted_iota(jnp.int32, (PAIR_ROWS, REL_PAD), 1).astype(f32)
     ).astype(f32).astype(bf16)
@@ -134,29 +137,33 @@
     spread[...] = spread_f.astype(bf16)
     spread_t[...] = spread_f.T.astype(bf16)
 
-    def core_step(src, side, q):
+    def core_step(src, core_of, q):
         row = pl.multiple_of(q * 512, 512)
         parts = [
             mm(spread[...], src[pl.ds(row + 256 * e, 256), :]).reshape(64, 8, 256)
             for e in range(2)
         ]
-        at = 64 * (2 * (q // 4) + side) + 16 * (q % 4)
+        at = 64 * (2 * (q // 4) + core_of) + 16 * (q % 4)
         cores[:, pl.ds(pl.multiple_of(at, 16), 16), :] = jnp.concatenate(parts, axis=1).astype(bf16)
 
-    for fetch, src, side in ((fetch_mine, mine_here, co), (fetch_other, other_here, 1 - co)):
+    for fetch, src, core_of in ((fetch_mine, mine_here, co), (fetch_other, other_here, 1 - co)):
         fetch.wait()
 
         @pl.loop(0, 8, unroll=4)
-        def _(q, src=src, side=side):
-            core_step(src, side, q)
-
-    for s in range(GROUP):
-        heads[s] = given[s][0:256, :]
-        tails[s] = given[s][256:512, :]
+        def _(q, src=src, core_of=core_of):
+            core_step(src, core_of, q)
+
+    heads[0] = own_heads[...]
+    tails[0] = own_tails[...]
+    for s in range(1, GROUP):
+        heads[s] = given[s][0:256, :].astype(f32)
+        tails[s] = given[s][256:512, :].astype(f32)
+    which = lax.broadcasted_iota(jnp.int32, (16, 256), 0)
 
     row = lax.broadcasted_iota(jnp.int32, (TILE, 256), 0)
-    half = pl.multiple_of((member // 2) * 128, 128)
-    odd = member % 2 == 1
+    near = pl.multiple_of(side * 128, 128)
+    far = pl.multiple_of((1 - side) * 128, 128)
+    even = (lax.broadcasted_iota(jnp.int32, (256, 128), 1) // 8) % 2 == 0
 
     def round_step(k, last):
         parts = [meta[3 + k * GROUP + (member ^ s)] for s in range(GROUP)]
@@ -164,7 +171,8 @@
         for s in slots:
             tails_low[s] = tails[parts[s] ^ member].astype(bf16)
             heads_low[s] = heads[s].astype(bf16)
-            heads_part[s] = heads[s, :, pl.ds(half, 128)].T.astype(bf16)
+            turned = jnp.where(even, heads[s, :, pl.ds(near, 128)], heads[s, :, pl.ds(far, 128)]).T
+            heads_part[s] = jnp.where(co == 1, turned[64:], turned[:64]).astype(bf16)
 
         def at(s, i, j):
             return ((s * 2 + i) * GROUP + parts[s]) * 2 + j
@@ -177,7 +185,11 @@
                         bf16
                     )
         for s in slots:
-            positive = given[s][pl.ds(512 + parts[s], 1), :].astype(jnp.int32)
+            positive = jnp.sum(
+                jnp.where(which == parts[s], given[s][512:528, :].astype(f32), 0.0),
+                axis=0,
+                keepdims=True,
+            ).astype(jnp.int32)
             row_loss = None
             for j in range(2):
                 score = mm_nt(tails_low[s, TILE * j : TILE * j + TILE, :], rel_core[s, j])
@@ -205,8 +217,7 @@
             for i in range(2):
                 rows = slice(TILE * i, TILE * i + TILE)
                 for j in range(2):
-                    outer = mm(heads_part[s, :, rows], grad_relcore[s, j, rows, :])
-                    grads[at(s, i, j)] = jnp.where(odd, outer[64:], outer[:64])
+                    grads[at(s, i, j)] = mm(heads_part[s, :, rows], grad_relcore[s, j, rows, :])
         for s in slots[:1] if last else slots:
             for i in range(2):
                 rows = slice(TILE * i, TILE * i + TILE)
@@ -232,9 +243,11 @@
     for e in range(8):
         low = grads[:, 8 * e : 8 * e + 8, :].reshape(512, 256).astype(bf16)
         part = mm(spread_t[...], low).astype(bf16)
+        first = (side ^ (e % 2)) * 16 + (e // 2) * 4
         for d in range(4):
-            out_pay[4 * e + d, 0:64, :] = part[64 * d : 64 * d + 64, :]
-        own_core = mine_here[pl.ds(pl.multiple_of(xl * 2048 + 256 * e, 256), 256), :]
+            out_pay[first + d, 0:64, :] = part[64 * d : 64 * d + 64, :]
+        part_at = (side ^ (e % 2)) * 2048 + 256 * e
+        own_core = mine_here[pl.ds(pl.multiple_of(part_at, 256), 256), :]
         total = total + mm_nt(low, own_core)
     wide = jnp.sum(jnp.where(on_row, total.reshape(64, 8, 256), 0.0), axis=1)
     folded = wide[:, :128] + wide[:, 128:]
@@ -242,14 +255,12 @@
     folded = folded + pltpu.roll(folded, 32, 1)
     lanes = lax.broadcasted_iota(jnp.int32, (16, 128), 1)
     packed = jnp.zeros((16, 128), f32)
-    names = jnp.zeros((16, 128), f32)
+    tags = jnp.zeros((16, 128), f32)
     for q in range(4):
-        own_ids = given[q][528:544, 0:1]
-        high = jnp.floor(own_ids * (1.0 / 256.0))
-        rest = own_ids - 256.0 * high
+        high, rest = names[q][:, 0:1], names[q][:, 1:2]
         packed = jnp.where(lanes // 32 == q, folded[16 * q : 16 * q + 16, :], packed)
-        names = jnp.where(lanes == 32 * q, high, jnp.where(lanes == 32 * q + 1, rest, names))
-    tag = jnp.concatenate([packed, names], axis=1).astype(bf16)
+        tags = jnp.where(lanes == 32 * q, high, jnp.where(lanes == 32 * q + 1, rest, tags))
+    tag = jnp.concatenate([packed, tags], axis=1).astype(bf16)
     for d in range(32):
         out_pay[d, 64:80, :] = tag
 
@@ -288,6 +299,19 @@
     out_rel[...] = total[:, : out_rel.shape[1]]
 
 
+def near_groups():
+    return [
+        [
+            (((x * 2 + c) * 4 + z) * 2 + (x ^ w)) * 4 + y
+            for x in range(2)
+            for z in range(4)
+            for y in range(4)
+        ]
+        for w in range(2)
+        for c in range(2)
+    ]
+
+
 def exchange(value, axes, step):
     size = lax.axis_size(axes)
     return lax.ppermute(value, axes, [(i, i ^ step) for i in range(size)])
@@ -310,13 +334,13 @@
 ):
     member = lax.axis_index(MEMBERS)
     co = lax.axis_index("co")
-    xl = lax.axis_index("xl")
+    side = lax.axis_index("xl") ^ lax.axis_index("xh")
     rel_count = relation_table.shape[0]
 
     own, low = pl.pallas_call(
         prepare_kernel,
         out_shape=(
-            jax.ShapeDtypeStruct((544, DE), f32),
+            jax.ShapeDtypeStruct((544, DE), bf16),
             jax.ShapeDtypeStruct((64, 64, DE), bf16),
         ),
         in_specs=[pl.BlockSpec(memory_space=pl.ANY)] * 5,
@@ -325,6 +349,7 @@
             pltpu.VMEM((GROUP, 256), jnp.int32),
             pltpu.VMEM((2, 8), jnp.int32),
             pltpu.VMEM((64, DE), f32),
+            pltpu.VMEM((544, DE), f32),
             pltpu.VMEM((64, 64, DE), bf16),
             pltpu.SemaphoreType.DMA((6,)),
         ],
@@ -339,7 +364,7 @@
     group = [own, beside, across, exchange(across, "co", 1)]
 
     meta = jnp.concatenate(
-        [jnp.stack([member, co, xl]).astype(jnp.int32), partner_table.reshape(-1)]
+        [jnp.stack([member, co, side]).astype(jnp.int32), partner_table.reshape(-1)]
     )
     head_now, tail_now, loss_now, pay = pl.pallas_call(
         train_kernel,
@@ -351,7 +376,7 @@
         ),
         in_specs=[pl.BlockSpec(memory_space=pltpu.SMEM)]
         + [pl.BlockSpec(memory_space=pl.ANY)] * 2
-        + vmem(5),
+        + vmem(7),
         out_specs=tuple(vmem(4)),
         scratch_shapes=[
             pltpu.VMEM((DR, REL_PAD), bf16),
@@ -361,7 +386,7 @@
             pltpu.VMEM((64, 64, 256), f32),
             pltpu.VMEM((GROUP, 256, DE), f32),
             pltpu.VMEM((GROUP, 256, DE), bf16),
-            pltpu.VMEM((GROUP, 128, DE), bf16),
+            pltpu.VMEM((GROUP, 64, DE), bf16),
             pltpu.VMEM((GROUP, 256, DE), f32),
             pltpu.VMEM((GROUP, 256, DE), bf16),
             pltpu.VMEM((GROUP, 2, 256, DE), bf16),
@@ -372,9 +397,11 @@
             pltpu.SemaphoreType.DMA((2,)),
         ],
         compiler_params=pltpu.CompilerParams(vmem_limit_bytes=48 * 1024 * 1024),
-    )(meta, mine, other, *group, relation_table.T)
-
-    got = lax.all_to_all(pay, GROUPS, split_axis=0, concat_axis=0, tiled=True)
+    )(meta, mine, other, head_vectors, tail_vectors, *group, relation_table.T)
+
+    got = lax.all_to_all(
+        pay, AXES, split_axis=0, concat_axis=0, tiled=True, axis_index_groups=near_groups()
+    )
     own_grad, square, rel_part = pl.pallas_call(
         sum_kernel,
         out_shape=(

time: 124 us -> 116 us (0.935)
  waiting for transfers between devices: 38.8 us -> 32 us
    ppermute x7, waiting for transfers between devices: 38.8 us -> 32 us  [exchange(): return lax.ppermute(value, axes, [(i, i ^ step) for i in range(size)])]
where the time goes in v3:
time: 116 us
  blocking collectives  41.7 us (36%)
  waiting for transfers between devices  32 us (28%)
  Pallas kernels  21 us (18%)
  starting transfers between devices  19.3 us (17%)
    ppermute x7, waiting for transfers between devices, exchange(): return lax.ppermute(value, axes, [(i, i ^ step) for i in range(size)])  32 us
    all_to_all x1, blocking collectives, body(): lax.all_to_all(pay, AXES, split_axis=0, concat_axis=0, tiled=True, axis_i...  28.5 us
    pallas_call x1, Pallas kernels, body(): pl.pallas_call(train_kernel, out_shape=(jax.ShapeDtypeStruct((256, DE), f...  15.5 us
    all_to_all x1, blocking collectives, body(): lax.all_to_all(square, AXES, split_axis=0, concat_axis=0, tiled=True)  13.1 us
    all_to_all x1, starting transfers between devices, body(): lax.all_to_all(low, CHIPS, split_axis=0, concat_axis=0, tiled=True)  12.1 us
    ppermute x7, starting transfers between devices, exchange(): return lax.ppermute(value, axes, [(i, i ^ step) for i in range(size)])  7.2 us
    pallas_call x1, Pallas kernels, body(): pl.pallas_call(prepare_kernel, out_shape=(jax.ShapeDtypeStruct((544, DE),...  3.19 us
  transfers between devices with their start and end apart: 8, of which 3 were waited for; matrix products, arithmetic and copies ran while one was open for 0% of the time, Pallas kernels for 0%

profile of v3, /device:TPU:1, one launch (start us, length us, event | category | flops | bytes accessed | tf_op | source)
XLA Modules:
  0.0 115.9 jit_solution(14018403414462041715)
XLA Ops:
  0.6 3.2 %shard_map.144 = (bf16[544,256]{1,0:T(8,128)(2,1)}, bf16[64,64,256]{2,1,0:T(8,128)(2,1)}) custom-call(f32[256,256]{1,0:T(8,128)} %own_heads.1, f32[256,256]{1,0:T(8,128)} %own_tails.1, s32[4,256]{1,0:T(4,128)} %bitcast.17, s32[2,8]{1,0:T(2,128)} %tiles.1, f32[64,256]{1,0:T(8,128)} %core.3), custom_call_target="tpu_custom_call" | custom-call | tf_op jit(solution)/shard_map/pallas_call | solution.py:340
  3.8 0.0 copy-start.2
  3.8 0.0 copy-start.7
  3.8 0.0 copy-start
  3.9 0.0 copy-start.1
  3.9 12.1 %all-to-all-start = ((bf16[64,64,256]{2,1,0:T(8,128)(2,1)}), bf16[64,64,256]{2,1,0:T(8,128)(2,1)S(1)}, u32[]{:S(2)}, u32[]{:S(2)}) async-start(bf16[64,64,256]{2,1,0:T(8,128)(2,1)} %get-tuple-element.22), calls=%async_computation | async-start | bytes 4194304 | tf_op jit(solution)/shard_map/all_to_all | solution.py:361
  16.0 0.0 copy-done.2
  16.0 1.2 %collective-permute-start = (bf16[544,256]{1,0:T(8,128)(2,1)S(1)}, bf16[544,256]{1,0:T(8,128)(2,1)S(1)}, u32[]{:S(2)}, u32[]{:S(2)}) collective-permute-start(bf16[544,256]{1,0:T(8,128)(2,1)S(1)} %copy-done.2), channel_id=1, source_target_pairs={{0,64},{64,0},{1,65},{65,1},{2,66},{66,2},{3,67},{67,3},{4,68},{68... | collective-permute-start | bytes 835592 | tf_op jit(solution)/shard_map/ppermute | solution.py:317
  17.2 27.9 %collective-permute-done.d2 = bf16[544,256]{1,0:T(8,128)(2,1)S(1)} collective-permute-done((bf16[544,256]{1,0:T(8,128)(2,1)S(1)}, bf16[544,256]{1,0:T(8,128)(2,1)S(1)}, u32[]{:S(2)}, u32[]{:S(2)}) %collective-permute-start) | collective-permute-done | bytes 278560 | tf_op jit(solution)/shard_map/ppermute | solution.py:317
  45.1 0.0 all-to-all-done
  45.1 1.9 %collective-permute-start.1 = (bf16[4096,256]{1,0:T(8,128)(2,1)S(1)}, bf16[4096,256]{1,0:T(8,128)(2,1)}, u32[]{:S(2)}, u32[]{:S(2)}) collective-permute-start(bf16[4096,256]{1,0:T(8,128)(2,1)S(1)} %bitcast.12), channel_id=1, source_target_pairs={{0,32},{32,0},{1,33},{33,1},{2,34},{34,2},{3,35},{35,3},{4,36},{36... | collective-permute-start | bytes 6291464 | tf_op jit(solution)/shard_map/ppermute | solution.py:317
  47.0 0.0 collective-permute-start.2
  47.0 0.5 collective-permute-start.3
  47.5 0.0 copy-done.7
  47.5 0.1 reshape.22
  47.6 0.1 pad_add_fusion.meta
  47.7 3.8 %collective-permute-done.2.d1 = bf16[544,256]{1,0:T(8,128)(2,1)S(1)} collective-permute-done((bf16[544,256]{1,0:T(8,128)(2,1)S(1)}, bf16[544,256]{1,0:T(8,128)(2,1)S(1)}, u32[]{:S(2)}, u32[]{:S(2)}) %collective-permute-start.2) | collective-permute-done | bytes 278560 | tf_op jit(solution)/shard_map/ppermute | solution.py:317
  51.5 0.3 collective-permute-done.3.d3
  51.7 0.0 collective-permute-done.1.other
  51.7 0.0 copy-done
  51.7 0.0 copy-done.1
  51.7 0.0 copy-start.4
  51.8 0.9 copy-done.4
  52.7 15.5 %shard_map.145 = (f32[256,256]{1,0:T(8,128)}, f32[256,256]{1,0:T(8,128)}, f32[4,256]{1,0:T(4,128)}, bf16[32,80,256]{2,1,0:T(8,128)(2,1)S(1)}) custom-call(s32[19]{0:T(128)S(1)} %pad_add_fusion.meta, bf16[4096,256]{1,0:T(8,128)(2,1)S(1)} %bitcast.13, bf16[4096,256]{1,0:T(8,128)(2,1)} %collective-permute-done.1.other, f32[256,256]{1,0:T(8,128)S(1)} %copy-done, ...), custom_call_target="tpu_custom_call" | custom-call | tf_op jit(solution)/shard_map/pallas_call | solution.py:369
  68.1 0.0 copy-start.3
  68.2 0.0 copy-start.5
  68.2 0.0 copy-start.6
  68.2 28.5 %all_to_all.21.got = bf16[32,80,256]{2,1,0:T(8,128)(2,1)S(1)} all-to-all(bf16[32,80,256]{2,1,0:T(8,128)(2,1)S(1)} %get-tuple-element.29), channel_id=1, replica_groups={{0,1,2,3,8,9,10,11,16,17,18,19,24,25,26,27,68,69,70,71,76,77,78,79,84,8..., dimensions={0} | all-to-all | bytes 2621440 | tf_op jit(solution)/shard_map/all_to_all | solution.py:402
  96.7 1.5 %shard_map.146 = (f32[64,256]{1,0:T(8,128)S(1)}, f32[128,128]{1,0:T(8,128)S(1)}, f32[32,1408]{1,0:T(8,128)S(1)}) custom-call(bf16[32,80,256]{2,1,0:T(8,128)(2,1)S(1)} %all_to_all.21.got), custom_call_target="tpu_custom_call" | custom-call | tf_op jit(solution)/shard_map/pallas_call | solution.py:405
  98.2 0.7 collective-permute-start.6
  98.9 2.9 %collective-permute-start.5 = (f32[32,1408]{1,0:T(8,128)S(1)}, f32[32,1408]{1,0:T(8,128)S(1)}, u32[]{:S(2)}, u32[]{:S(2)}) collective-permute-start(f32[32,1408]{1,0:T(8,128)S(1)} %get-tuple-element.32.r0), channel_id=1, source_target_pairs={{0,64},{32,96},{64,0},{96,32},{1,65},{33,97},{65,1},{97,33},{2,66}... | collective-permute-start | bytes 540680 | tf_op jit(solution)/shard_map/ppermute | solution.py:317
  101.8 0.0 collective-permute-start.4
  101.8 13.1 %all_to_all.22 = f32[128,1,128]{2,1,0:T(1,128)S(1)} all-to-all(f32[128,1,128]{2,1,0:T(1,128)S(1)} %bitcast.16), channel_id=1, replica_groups=mesh['xl'=2,'co'=2,'z'=4,'xh'=2,'y'=4] {'xl','co','z','xh','y'}, dimensions={0} | all-to-all | bytes 131072 | tf_op jit(solution)/shard_map/all_to_all | solution.py:417
  114.9 0.0 collective-permute-done.6.r3
  114.9 0.0 collective-permute-done.5.r2
  114.9 0.0 collective-permute-done.4.r1
  114.9 0.0 copy-done.3
  114.9 0.0 copy-done.5
  114.9 0.0 copy-done.6
  115.0 0.9 shard_map.147
Async XLA Ops:
  3.8 12.2 %copy-start.2 = (bf16[544,256]{1,0:T(8,128)(2,1)S(1)}, bf16[544,256]{1,0:T(8,128)(2,1)}, u32[]{:S(2)}) copy-start(bf16[544,256]{1,0:T(8,128)(2,1)} %get-tuple-element.23.d0) | copy-start | bytes 835588
  3.8 43.7 %copy-start.7 = (s32[1,4,4]{2,1,0:T(4,128)S(1)}, s32[1,4,4]{2,1,0:T(4,128)}, u32[]{:S(2)}) copy-start(s32[1,4,4]{2,1,0:T(4,128)} %param.17) | copy-start | bytes 196
  3.8 47.9 %copy-start = (f32[256,256]{1,0:T(8,128)S(1)}, f32[256,256]{1,0:T(8,128)}, u32[]{:S(2)}) copy-start(f32[256,256]{1,0:T(8,128)} %own_heads.1) | copy-start | bytes 786436
  3.9 47.9 %copy-start.1 = (f32[256,256]{1,0:T(8,128)S(1)}, f32[256,256]{1,0:T(8,128)}, u32[]{:S(2)}) copy-start(f32[256,256]{1,0:T(8,128)} %own_tails.1) | copy-start | bytes 786436
  3.9 41.3 %all-to-all-start = ((bf16[64,64,256]{2,1,0:T(8,128)(2,1)}), bf16[64,64,256]{2,1,0:T(8,128)(2,1)S(1)}, u32[]{:S(2)}, u32[]{:S(2)}) async-start(bf16[64,64,256]{2,1,0:T(8,128)(2,1)} %get-tuple-element.22), calls=%async_computation | async-start | bytes 4194304 | tf_op jit(solution)/shard_map/all_to_all | solution.py:361
  16.0 29.1 %collective-permute-start = (bf16[544,256]{1,0:T(8,128)(2,1)S(1)}, bf16[544,256]{1,0:T(8,128)(2,1)S(1)}, u32[]{:S(2)}, u32[]{:S(2)}) collective-permute-start(bf16[544,256]{1,0:T(8,128)(2,1)S(1)} %copy-done.2), channel_id=1, source_target_pairs={{0,64},{64,0},{1,65},{65,1},{2,66},{66,2},{3,67},{67,3},{4,68},{68... | collective-permute-start | bytes 835592 | tf_op jit(solution)/shard_map/ppermute | solution.py:317
  45.1 6.6 %collective-permute-start.1 = (bf16[4096,256]{1,0:T(8,128)(2,1)S(1)}, bf16[4096,256]{1,0:T(8,128)(2,1)}, u32[]{:S(2)}, u32[]{:S(2)}) collective-permute-start(bf16[4096,256]{1,0:T(8,128)(2,1)S(1)} %bitcast.12), channel_id=1, source_target_pairs={{0,32},{32,0},{1,33},{33,1},{2,34},{34,2},{3,35},{35,3},{4,36},{36... | collective-permute-start | bytes 6291464 | tf_op jit(solution)/shard_map/ppermute | solution.py:317
  47.0 4.4 %collective-permute-start.2 = (bf16[544,256]{1,0:T(8,128)(2,1)S(1)}, bf16[544,256]{1,0:T(8,128)(2,1)S(1)}, u32[]{:S(2)}, u32[]{:S(2)}) collective-permute-start(bf16[544,256]{1,0:T(8,128)(2,1)S(1)} %copy-done.2), channel_id=1, source_target_pairs={{0,32},{32,0},{1,33},{33,1},{2,34},{34,2},{3,35},{35,3},{4,36},{36... | collective-permute-start | bytes 835592 | tf_op jit(solution)/shard_map/ppermute | solution.py:317
  47.0 4.7 %collective-permute-start.3 = (bf16[544,256]{1,0:T(8,128)(2,1)S(1)}, bf16[544,256]{1,0:T(8,128)(2,1)}, u32[]{:S(2)}, u32[]{:S(2)}) collective-permute-start(bf16[544,256]{1,0:T(8,128)(2,1)S(1)} %collective-permute-done.d2), channel_id=1, source_target_pairs={{0,32},{32,0},{1,33},{33,1},{2,34},{34,2},{3,35},{35,3},{4,36},{36... | collective-permute-start | bytes 835592 | tf_op jit(solution)/shard_map/ppermute | solution.py:317
  51.7 0.9 copy-start.4
  68.1 46.8 %copy-start.3 = (f32[64,256]{1,0:T(8,128)S(1)}, f32[64,256]{1,0:T(8,128)}, u32[]{:S(2)}) copy-start(f32[64,256]{1,0:T(8,128)} %core.3) | copy-start | bytes 196612
  68.2 46.8 %copy-start.5 = (f32[64,256]{1,0:T(8,128)S(1)}, f32[64,256]{1,0:T(8,128)}, u32[]{:S(2)}) copy-start(f32[64,256]{1,0:T(8,128)} %moment.1) | copy-start | bytes 196612
  68.2 46.8 %copy-start.6 = (f32[64,256]{1,0:T(8,128)S(1)}, f32[64,256]{1,0:T(8,128)}, u32[]{:S(2)}) copy-start(f32[64,256]{1,0:T(8,128)} %second.1) | copy-start | bytes 196612
  98.2 16.8 %collective-permute-start.6 = (f32[32,1408]{1,0:T(8,128)S(1)}, f32[32,1408]{1,0:T(8,128)S(1)}, u32[]{:S(2)}, u32[]{:S(2)}) collective-permute-start(f32[32,1408]{1,0:T(8,128)S(1)} %get-tuple-element.32.r0), channel_id=1, source_target_pairs={{0,96},{32,64},{64,32},{96,0},{1,97},{33,65},{65,33},{97,1},{2,98}... | collective-permute-start | bytes 540680 | tf_op jit(solution)/shard_map/ppermute | solution.py:317
  98.9 16.0 %collective-permute-start.5 = (f32[32,1408]{1,0:T(8,128)S(1)}, f32[32,1408]{1,0:T(8,128)S(1)}, u32[]{:S(2)}, u32[]{:S(2)}) collective-permute-start(f32[32,1408]{1,0:T(8,128)S(1)} %get-tuple-element.32.r0), channel_id=1, source_target_pairs={{0,64},{32,96},{64,0},{96,32},{1,65},{33,97},{65,1},{97,33},{2,66}... | collective-permute-start | bytes 540680 | tf_op jit(solution)/shard_map/ppermute | solution.py:317
  101.8 13.1 %collective-permute-start.4 = (f32[32,1408]{1,0:T(8,128)S(1)}, f32[32,1408]{1,0:T(8,128)S(1)}, u32[]{:S(2)}, u32[]{:S(2)}) collective-permute-start(f32[32,1408]{1,0:T(8,128)S(1)} %get-tuple-element.32.r0), channel_id=1, source_target_pairs={{0,32},{32,0},{64,96},{96,64},{1,33},{33,1},{65,97},{97,65},{2,34}... | collective-permute-start | bytes 540680 | tf_op jit(solution)/shard_map/ppermute | solution.py:317

commit v4 on v3

--- a/solution.py
+++ b/solution.py
@@ -12,6 +12,7 @@
 PAIR_ROWS = 64
 REL_PAD = 1408
 WHOLE = 60 * 1024 * 1024
+PREPARE = 60 * 1024 * 1024
 
 entity_rate = 4.0
 core_rate = 0.001
@@ -39,25 +40,32 @@
     return lax.dot_general(a, b, (((0,), (0,)), ((), ())), preferred_element_type=f32)
 
 
-def prepare_kernel(
-    heads, tails, positive, tiles, core, out_own, out_core, hits, names, rows, both, wide, sems
-):
+def copies_kernel(core, out_core, rows, wide, sems):
+    load = pltpu.make_async_copy(core, rows, sems.at[0])
+    load.start()
+    load.wait()
+    low = rows[...].astype(bf16)
+    moves = []
+    for q in range(4):
+        for d in range(16 * q, 16 * q + 16):
+            wide[d] = low
+        part = slice(16 * q, 16 * q + 16)
+        moves.append(pltpu.make_async_copy(wide.at[part], out_core.at[part], sems.at[1 + q]))
+        moves[-1].start()
+    for move in moves:
+        move.wait()
+
+
+def prepare_kernel(heads, tails, positive, tiles, out_own, hits, names, both, sems):
     moves = [
-        pltpu.make_async_copy(core, rows, sems.at[0]),
-        pltpu.make_async_copy(heads, both.at[0:256, :], sems.at[1]),
-        pltpu.make_async_copy(tails, both.at[256:512, :], sems.at[2]),
-        pltpu.make_async_copy(tiles, names, sems.at[3]),
-        pltpu.make_async_copy(positive, hits, sems.at[4]),
+        pltpu.make_async_copy(heads, both.at[0:256, :], sems.at[0]),
+        pltpu.make_async_copy(tails, both.at[256:512, :], sems.at[1]),
+        pltpu.make_async_copy(tiles, names, sems.at[2]),
+        pltpu.make_async_copy(positive, hits, sems.at[3]),
     ]
     for move in moves:
         move.start()
-    moves[0].wait()
-    low = rows[...].astype(bf16)
-    for d in range(64):
-        wide[d] = low
-    spread_out = pltpu.make_async_copy(wide, out_core, sems.at[5])
-    spread_out.start()
-    for move in moves[1:]:
+    for move in moves:
         move.wait()
     pick = lax.broadcasted_iota(jnp.int32, (8, 8), 0) == lax.broadcasted_iota(
         jnp.int32, (8, 8), 1
@@ -71,7 +79,54 @@
         both[528 + 8 * i : 536 + 8 * i, 0:1] = high
         both[528 + 8 * i : 536 + 8 * i, 1:2] = column - 256.0 * high
     out_own[...] = both[...].astype(bf16)
-    spread_out.wait()
+
+
+def on_rows():
+    return (
+        lax.broadcasted_iota(jnp.int32, (64, 8, 256), 2) // DR
+        == lax.broadcasted_iota(jnp.int32, (64, 8, 256), 1)
+    )
+
+
+def core_step(spread, src, q):
+    row = pl.multiple_of(q * 512, 512)
+    parts = [
+        mm(spread[...], src[pl.ds(row + 256 * e, 256), :]).reshape(64, 8, 256) for e in range(2)
+    ]
+    return jnp.concatenate(parts, axis=1).astype(bf16)
+
+
+def form_kernel(mine, d0, d1, d2, d3, table, spread, spread_t, cores, table_low, marks, sems):
+    rel_count = table.shape[1]
+    moves = [
+        pltpu.make_async_copy(d.at[528:544, :], marks.at[s], sems.at[s])
+        for s, d in enumerate((d0, d1, d2, d3))
+    ]
+    for move in moves:
+        move.start()
+    table_low[...] = jnp.zeros_like(table_low)
+    table_low[:, 0:rel_count] = table[...].astype(bf16)
+    for move in moves:
+        move.wait()
+    names = marks[...].reshape(PAIR_ROWS, 256).astype(f32)
+    ids = names[:, 0:1] * 256.0 + names[:, 1:2]
+    hot = (
+        ids == lax.broadcasted_iota(jnp.int32, (PAIR_ROWS, REL_PAD), 1).astype(f32)
+    ).astype(f32).astype(bf16)
+    rel_low = mm_nt(hot, table_low[...]).astype(bf16)
+    copies = (
+        lax.broadcasted_iota(jnp.int32, (DR, 256), 1) % DR
+        == lax.broadcasted_iota(jnp.int32, (DR, 256), 0)
+    ).astype(f32).astype(bf16)
+    rel_wide = mm(rel_low, copies)
+    on_row = on_rows()
+    spread_f = jnp.where(on_row, rel_wide[:, None, :], 0.0).reshape(512, 256)
+    spread[...] = spread_f.astype(bf16)
+    spread_t[...] = spread_f.T.astype(bf16)
+
+    @pl.loop(0, 8, unroll=4)
+    def _(q):
+        cores[:, pl.ds(pl.multiple_of(16 * q, 16), 16), :] = core_step(spread, mine, q)
 
 
 def train_kernel(
@@ -84,14 +139,13 @@
     d1,
     d2,
     d3,
-    table,
+    spread,
+    spread_t,
+    formed,
     out_head,
     out_tail,
     out_loss,
     out_pay,
-    table_low,
-    spread,
-    spread_t,
     cores,
     grads,
     heads,
@@ -102,57 +156,35 @@
     rel_core,
     grad_relcore,
     slopes,
-    mine_here,
     other_here,
+    gathered,
     sems,
 ):
-    fetch_mine = pltpu.make_async_copy(mine, mine_here, sems.at[0])
-    fetch_other = pltpu.make_async_copy(other, other_here, sems.at[1])
-    fetch_mine.start()
+    fetch_other = pltpu.make_async_copy(other, other_here, sems.at[GROUP])
     fetch_other.start()
+    moves = [
+        pltpu.make_async_copy(d, gathered.at[s], sems.at[s]) for s, d in enumerate((d0, d1, d2, d3))
+    ]
+    for move in moves:
+        move.start()
     member = meta[0]
     co = meta[1]
     side = meta[2]
-    given = (d0, d1, d2, d3)
-    rel_count = table.shape[1]
-
-    table_low[...] = jnp.zeros_like(table_low)
-    table_low[:, 0:rel_count] = table[...].astype(bf16)
+    given = [gathered.at[s] for s in range(GROUP)]
+    on_row = on_rows()
+    for x in range(2):
+        at = pl.multiple_of(64 * (2 * x + co), 64)
+        cores[:, pl.ds(at, 64), :] = formed[:, 64 * x : 64 * x + 64, :]
+    fetch_other.wait()
+
+    @pl.loop(0, 8, unroll=4)
+    def _(q):
+        at = 64 * (2 * (q // 4) + 1 - co) + 16 * (q % 4)
+        cores[:, pl.ds(pl.multiple_of(at, 16), 16), :] = core_step(spread, other_here, q)
+
+    for move in moves:
+        move.wait()
     names = [d[528:544, 0:128].astype(f32) for d in given]
-    ids = jnp.concatenate([d[:, 0:1] * 256.0 + d[:, 1:2] for d in names], axis=0)
-    hot = (
-        ids == lax.broadcasted_iota(jnp.int32, (PAIR_ROWS, REL_PAD), 1).astype(f32)
-    ).astype(f32).astype(bf16)
-    rel_low = mm_nt(hot, table_low[...]).astype(bf16)
-    copies = (
-        lax.broadcasted_iota(jnp.int32, (DR, 256), 1) % DR
-        == lax.broadcasted_iota(jnp.int32, (DR, 256), 0)
-    ).astype(f32).astype(bf16)
-    rel_wide = mm(rel_low, copies)
-    on_row = (
-        lax.broadcasted_iota(jnp.int32, (64, 8, 256), 2) // DR
-        == lax.broadcasted_iota(jnp.int32, (64, 8, 256), 1)
-    )
-    spread_f = jnp.where(on_row, rel_wide[:, None, :], 0.0).reshape(512, 256)
-    spread[...] = spread_f.astype(bf16)
-    spread_t[...] = spread_f.T.astype(bf16)
-
-    def core_step(src, core_of, q):
-        row = pl.multiple_of(q * 512, 512)
-        parts = [
-            mm(spread[...], src[pl.ds(row + 256 * e, 256), :]).reshape(64, 8, 256)
-            for e in range(2)
-        ]
-        at = 64 * (2 * (q // 4) + core_of) + 16 * (q % 4)
-        cores[:, pl.ds(pl.multiple_of(at, 16), 16), :] = jnp.concatenate(parts, axis=1).astype(bf16)
-
-    for fetch, src, core_of in ((fetch_mine, mine_here, co), (fetch_other, other_here, 1 - co)):
-        fetch.wait()
-
-        @pl.loop(0, 8, unroll=4)
-        def _(q, src=src, core_of=core_of):
-            core_step(src, core_of, q)
-
     heads[0] = own_heads[...]
     tails[0] = own_tails[...]
     for s in range(1, GROUP):
@@ -247,7 +279,7 @@
         for d in range(4):
             out_pay[first + d, 0:64, :] = part[64 * d : 64 * d + 64, :]
         part_at = (side ^ (e % 2)) * 2048 + 256 * e
-        own_core = mine_here[pl.ds(pl.multiple_of(part_at, 256), 256), :]
+        own_core = mine[pl.ds(pl.multiple_of(part_at, 256), 256), :]
         total = total + mm_nt(low, own_core)
     wide = jnp.sum(jnp.where(on_row, total.reshape(64, 8, 256), 0.0), axis=1)
     folded = wide[:, :128] + wide[:, 128:]
@@ -337,31 +369,61 @@
     side = lax.axis_index("xl") ^ lax.axis_index("xh")
     rel_count = relation_table.shape[0]
 
-    own, low = pl.pallas_call(
+    low = pl.pallas_call(
+        copies_kernel,
+        out_shape=jax.ShapeDtypeStruct((64, 64, DE), bf16),
+        in_specs=[pl.BlockSpec(memory_space=pl.ANY)],
+        out_specs=pl.BlockSpec(memory_space=pl.ANY),
+        scratch_shapes=[
+            pltpu.VMEM((64, DE), f32),
+            pltpu.VMEM((64, 64, DE), bf16),
+            pltpu.SemaphoreType.DMA((5,)),
+        ],
+        compiler_params=pltpu.CompilerParams(vmem_limit_bytes=WHOLE),
+    )(core_tensor)
+    own = pl.pallas_call(
         prepare_kernel,
-        out_shape=(
-            jax.ShapeDtypeStruct((544, DE), bf16),
-            jax.ShapeDtypeStruct((64, 64, DE), bf16),
-        ),
-        in_specs=[pl.BlockSpec(memory_space=pl.ANY)] * 5,
-        out_specs=(pl.BlockSpec(memory_space=pltpu.VMEM), pl.BlockSpec(memory_space=pl.ANY)),
+        out_shape=jax.ShapeDtypeStruct((544, DE), bf16),
+        in_specs=[pl.BlockSpec(memory_space=pl.ANY)] * 4,
+        out_specs=pl.BlockSpec(memory_space=pltpu.VMEM),
         scratch_shapes=[
             pltpu.VMEM((GROUP, 256), jnp.int32),
             pltpu.VMEM((2, 8), jnp.int32),
-            pltpu.VMEM((64, DE), f32),
             pltpu.VMEM((544, DE), f32),
-            pltpu.VMEM((64, 64, DE), bf16),
-            pltpu.SemaphoreType.DMA((6,)),
+            pltpu.SemaphoreType.DMA((4,)),
         ],
-        compiler_params=pltpu.CompilerParams(vmem_limit_bytes=WHOLE),
-    )(head_vectors, tail_vectors, positive_tail.T, tile_relation, core_tensor)
+        compiler_params=pltpu.CompilerParams(vmem_limit_bytes=PREPARE),
+        cost_estimate=pl.CostEstimate(
+            flops=544 * 256, bytes_accessed=1024 * 1024, transcendentals=0
+        ),
+    )(head_vectors, tail_vectors, positive_tail.T, tile_relation)
     across = exchange(own, "xl", 1)
     beside = exchange(own, "co", 1)
 
     mine = lax.all_to_all(low, CHIPS, split_axis=0, concat_axis=0, tiled=True).reshape(4096, DE)
-    mine, across = lax.optimization_barrier((mine, across))
+    beyond = exchange(across, "co", 1)
+    mine, across, beside, beyond = lax.optimization_barrier((mine, across, beside, beyond))
     other = exchange(mine, "co", 1)
-    group = [own, beside, across, exchange(across, "co", 1)]
+    group = [own, beside, across, beyond]
+    spread, spread_t, formed = pl.pallas_call(
+        form_kernel,
+        out_shape=(
+            jax.ShapeDtypeStruct((512, DE), bf16),
+            jax.ShapeDtypeStruct((DE, 512), bf16),
+            jax.ShapeDtypeStruct((PAIR_ROWS, 128, DE), bf16),
+        ),
+        in_specs=vmem(1) + [pl.BlockSpec(memory_space=pl.ANY)] * 4 + vmem(1),
+        out_specs=tuple(vmem(3)),
+        scratch_shapes=[
+            pltpu.VMEM((DR, REL_PAD), bf16),
+            pltpu.VMEM((GROUP, 16, DE), bf16),
+            pltpu.SemaphoreType.DMA((GROUP,)),
+        ],
+        compiler_params=pltpu.CompilerParams(vmem_limit_bytes=24 * 1024 * 1024),
+        cost_estimate=pl.CostEstimate(
+            flops=2 * 512 * 256 * 4096, bytes_accessed=8 * 1024 * 1024, transcendentals=0
+        ),
+    )(mine, *group, relation_table.T)
 
     meta = jnp.concatenate(
         [jnp.stack([member, co, side]).astype(jnp.int32), partner_table.reshape(-1)]
@@ -375,13 +437,13 @@
             jax.ShapeDtypeStruct((32, 80, DE), bf16),
         ),
         in_specs=[pl.BlockSpec(memory_space=pltpu.SMEM)]
-        + [pl.BlockSpec(memory_space=pl.ANY)] * 2
-        + vmem(7),
+        + vmem(1)
+        + [pl.BlockSpec(memory_space=pl.ANY)]
+        + vmem(2)
+        + [pl.BlockSpec(memory_space=pl.ANY)] * 4
+        + vmem(3),
         out_specs=tuple(vmem(4)),
         scratch_shapes=[
-            pltpu.VMEM((DR, REL_PAD), bf16),
-            pltpu.VMEM((512, 256), bf16),
-            pltpu.VMEM((256, 512), bf16),
             pltpu.VMEM((64, 256, 256), bf16),
             pltpu.VMEM((64, 64, 256), f32),
             pltpu.VMEM((GROUP, 256, DE), f32),
@@ -393,11 +455,11 @@
             pltpu.VMEM((GROUP, 2, 256, DE), bf16),
             pltpu.VMEM((GROUP, 2, TILE, DE), bf16),
             pltpu.VMEM((4096, DE), bf16),
-            pltpu.VMEM((4096, DE), bf16),
-            pltpu.SemaphoreType.DMA((2,)),
+            pltpu.VMEM((GROUP, 544, DE), bf16),
+            pltpu.SemaphoreType.DMA((GROUP + 1,)),
         ],
-        compiler_params=pltpu.CompilerParams(vmem_limit_bytes=48 * 1024 * 1024),
-    )(meta, mine, other, head_vectors, tail_vectors, *group, relation_table.T)
+        compiler_params=pltpu.CompilerParams(vmem_limit_bytes=36 * 1024 * 1024),
+    )(meta, mine, other, head_vectors, tail_vectors, *group, spread, spread_t, formed)
 
     got = lax.all_to_all(
         pay, AXES, split_axis=0, concat_axis=0, tiled=True, axis_index_groups=near_groups()

time: 116 us -> 114 us (0.983)
  waiting for transfers between devices: 32 us -> 25.7 us
  Pallas kernels: 21 us -> 22.9 us
    ppermute x7, waiting for transfers between devices: 32 us -> 25.7 us  [exchange(): return lax.ppermute(value, axes, [(i, i ^ step) for i in range(size)])]
    pallas_call x1 -> x3, Pallas kernels: 3.19 us -> 6.31 us  [the longest x1 2.27 us: body(): pl.pallas_call(copies_kernel, out_shape=jax.ShapeDtypeStruct((64, 64, DE)...]
    pallas_call x1, Pallas kernels: 15.5 us -> 14.2 us  [body(): pl.pallas_call(train_kernel, out_shape=(jax.ShapeDtypeStruct((256, DE), f...]
  transfers between devices with their start and end apart: 8 -> 8, of which waited for: 3 -> 2; matrix products, arithmetic and copies ran while one was open for 0% -> 0% of each run, Pallas kernels for 0% -> 4%
where the time goes in v4:
time: 114 us
  blocking collectives  42.2 us (37%)
  waiting for transfers between devices  25.7 us (23%)
  Pallas kernels  22.9 us (20%)
  starting transfers between devices  20 us (18%)
  local copies, waits for them, and re-layouts  2 us (2%)
    all_to_all x1, blocking collectives, body(): lax.all_to_all(pay, AXES, split_axis=0, concat_axis=0, tiled=True, axis_i...  29.1 us
    ppermute x7, waiting for transfers between devices, exchange(): return lax.ppermute(value, axes, [(i, i ^ step) for i in range(size)])  25.7 us
    pallas_call x1, Pallas kernels, body(): pl.pallas_call(train_kernel, out_shape=(jax.ShapeDtypeStruct((256, DE), f...  14.2 us
    all_to_all x1, blocking collectives, body(): lax.all_to_all(square, AXES, split_axis=0, concat_axis=0, tiled=True)  13.1 us
    all_to_all x1, starting transfers between devices, body(): lax.all_to_all(low, CHIPS, split_axis=0, concat_axis=0, tiled=True)  12 us
    ppermute x7, starting transfers between devices, exchange(): return lax.ppermute(value, axes, [(i, i ^ step) for i in range(size)])  8 us
  transfers between devices with their start and end apart: 8, of which 2 were waited for; matrix products, arithmetic and copies ran while one was open for 0% of the time, Pallas kernels for 4%

profile of v4, /device:TPU:1, one launch (start us, length us, event | category | flops | bytes accessed | tf_op | source)
XLA Modules:
  0.0 113.6 jit_solution(1172019532362912029)
XLA Ops:
  0.6 2.3 %shard_map.144 = bf16[64,64,256]{2,1,0:T(8,128)(2,1)} custom-call(f32[64,256]{1,0:T(8,128)} %core.3), custom_call_target="tpu_custom_call" | custom-call | tf_op jit(solution)/shard_map/pallas_call | solution.py:372
  2.9 0.0 copy-start.8
  2.9 12.0 %all-to-all-start = ((bf16[64,64,256]{2,1,0:T(8,128)(2,1)}), bf16[64,64,256]{2,1,0:T(8,128)(2,1)S(1)}, u32[]{:S(2)}, u32[]{:S(2)}) async-start(bf16[64,64,256]{2,1,0:T(8,128)(2,1)} %shard_map.144), calls=%async_computation | async-start | bytes 4194304 | tf_op jit(solution)/shard_map/all_to_all | solution.py:403
  14.9 0.0 copy-start.2
  14.9 0.0 copy-start.3
  14.9 1.9 %shard_map.145.d0 = bf16[544,256]{1,0:T(8,128)(2,1)} custom-call(f32[256,256]{1,0:T(8,128)} %own_heads.1, f32[256,256]{1,0:T(8,128)} %own_tails.1, s32[4,256]{1,0:T(4,128)} %bitcast.18, s32[2,8]{1,0:T(2,128)} %tiles.1), custom_call_target="tpu_custom_call" | custom-call | flops 139264 | bytes 1048576 | tf_op jit(solution)/shard_map/pallas_call | solution.py:384
  16.9 1.2 %collective-permute-start = (bf16[544,256]{1,0:T(8,128)(2,1)}, bf16[544,256]{1,0:T(8,128)(2,1)S(1)}, u32[]{:S(2)}, u32[]{:S(2)}) collective-permute-start(bf16[544,256]{1,0:T(8,128)(2,1)} %shard_map.145.d0), channel_id=1, source_target_pairs={{0,64},{64,0},{1,65},{65,1},{2,66},{66,2},{3,67},{67,3},{4,68},{68... | collective-permute-start | bytes 835592 | tf_op jit(solution)/shard_map/ppermute | solution.py:349
  18.1 1.5 %collective-permute-start.1 = (bf16[544,256]{1,0:T(8,128)(2,1)}, bf16[544,256]{1,0:T(8,128)(2,1)S(1)}, u32[]{:S(2)}, u32[]{:S(2)}) collective-permute-start(bf16[544,256]{1,0:T(8,128)(2,1)} %shard_map.145.d0), channel_id=1, source_target_pairs={{0,32},{32,0},{1,33},{33,1},{2,34},{34,2},{3,35},{35,3},{4,36},{36... | collective-permute-start | bytes 835592 | tf_op jit(solution)/shard_map/ppermute | solution.py:349
  19.6 24.5 %collective-permute-done.d2 = bf16[544,256]{1,0:T(8,128)(2,1)S(1)} collective-permute-done((bf16[544,256]{1,0:T(8,128)(2,1)}, bf16[544,256]{1,0:T(8,128)(2,1)S(1)}, u32[]{:S(2)}, u32[]{:S(2)}) %collective-permute-start) | collective-permute-done | bytes 278560 | tf_op jit(solution)/shard_map/ppermute | solution.py:349
  44.1 1.9 %collective-permute-start.2 = (bf16[544,256]{1,0:T(8,128)(2,1)S(1)}, bf16[544,256]{1,0:T(8,128)(2,1)S(1)}, u32[]{:S(2)}, u32[]{:S(2)}) collective-permute-start(bf16[544,256]{1,0:T(8,128)(2,1)S(1)} %collective-permute-done.d2), channel_id=1, source_target_pairs={{0,32},{32,0},{1,33},{33,1},{2,34},{34,2},{3,35},{35,3},{4,36},{36... | collective-permute-start | bytes 835592 | tf_op jit(solution)/shard_map/ppermute | solution.py:349
  45.9 0.0 collective-permute-done.1.d1
  45.9 1.2 %collective-permute-done.2.d3 = bf16[544,256]{1,0:T(8,128)(2,1)S(1)} collective-permute-done((bf16[544,256]{1,0:T(8,128)(2,1)S(1)}, bf16[544,256]{1,0:T(8,128)(2,1)S(1)}, u32[]{:S(2)}, u32[]{:S(2)}) %collective-permute-start.2) | collective-permute-done | bytes 278560 | tf_op jit(solution)/shard_map/ppermute | solution.py:349
  47.1 0.0 all-to-all-done
  47.1 0.4 collective-permute-start.3
  47.5 0.0 copy-done.8
  47.5 0.1 reshape.22
  47.6 0.1 pad_add_fusion.meta
  47.7 0.0 copy-start
  47.7 1.0 copy-done
  48.6 0.0 copy-start.7
  48.6 0.9 copy-done.7
  49.5 0.0 copy-start.1
  49.5 2.1 %shard_map.146 = (bf16[512,256]{1,0:T(8,128)(2,1)S(1)}, bf16[256,512]{1,0:T(8,128)(2,1)S(1)}, bf16[64,128,256]{2,1,0:T(8,128)(2,1)S(1)}) custom-call(bf16[4096,256]{1,0:T(8,128)(2,1)S(1)} %bitcast.13, bf16[544,256]{1,0:T(8,128)(2,1)S(1)} %copy-done, bf16[544,256]{1,0:T(8,128)(2,1)S(1)} %collective-permute-done.1.d1, ...), custom_call_target="tpu_custom_call" | custom-call | flops 1073741824 | bytes 8388608 | tf_op jit(solution)/shard_map/pallas_call | solution.py:408
  51.7 0.0 collective-permute-done.3.other
  51.7 0.0 copy-done.2
  51.7 0.0 copy-done.3
  51.7 0.0 copy-done.1
  51.7 14.2 %shard_map.147 = (f32[256,256]{1,0:T(8,128)}, f32[256,256]{1,0:T(8,128)}, f32[4,256]{1,0:T(4,128)}, bf16[32,80,256]{2,1,0:T(8,128)(2,1)S(1)}) custom-call(s32[19]{0:T(128)S(1)} %pad_add_fusion.meta, bf16[4096,256]{1,0:T(8,128)(2,1)S(1)} %bitcast.14, bf16[4096,256]{1,0:T(8,128)(2,1)} %collective-permute-done.3.other, f32[256,256]{1,0:T(8,128)S(1)} %copy-done.2, ...), custom_call_target="tpu_custom_call" | custom-call | tf_op jit(solution)/shard_map/pallas_call | solution.py:431
  65.9 0.0 copy-start.4
  65.9 0.0 copy-start.5
  66.0 0.0 copy-start.6
  66.0 29.1 %all_to_all.21.got = bf16[32,80,256]{2,1,0:T(8,128)(2,1)S(1)} all-to-all(bf16[32,80,256]{2,1,0:T(8,128)(2,1)S(1)} %get-tuple-element.35), channel_id=1, replica_groups={{0,1,2,3,8,9,10,11,16,17,18,19,24,25,26,27,68,69,70,71,76,77,78,79,84,8..., dimensions={0} | all-to-all | bytes 2621440 | tf_op jit(solution)/shard_map/all_to_all | solution.py:464
  95.0 1.5 %shard_map.148 = (f32[64,256]{1,0:T(8,128)S(1)}, f32[128,128]{1,0:T(8,128)S(1)}, f32[32,1408]{1,0:T(8,128)S(1)}) custom-call(bf16[32,80,256]{2,1,0:T(8,128)(2,1)S(1)} %all_to_all.21.got), custom_call_target="tpu_custom_call" | custom-call | tf_op jit(solution)/shard_map/pallas_call | solution.py:467
  96.5 0.1 collective-permute-start.6
  96.7 2.9 %collective-permute-start.5 = (f32[32,1408]{1,0:T(8,128)S(1)}, f32[32,1408]{1,0:T(8,128)S(1)}, u32[]{:S(2)}, u32[]{:S(2)}) collective-permute-start(f32[32,1408]{1,0:T(8,128)S(1)} %get-tuple-element.38.r0), channel_id=1, source_target_pairs={{0,64},{32,96},{64,0},{96,32},{1,65},{33,97},{65,1},{97,33},{2,66}... | collective-permute-start | bytes 540680 | tf_op jit(solution)/shard_map/ppermute | solution.py:349
  99.6 0.0 collective-permute-start.4
  99.6 13.1 %all_to_all.22 = f32[128,1,128]{2,1,0:T(1,128)S(1)} all-to-all(f32[128,1,128]{2,1,0:T(1,128)S(1)} %bitcast.16), channel_id=1, replica_groups=mesh['xl'=2,'co'=2,'z'=4,'xh'=2,'y'=4] {'xl','co','z','xh','y'}, dimensions={0} | all-to-all | bytes 131072 | tf_op jit(solution)/shard_map/all_to_all | solution.py:479
  112.7 0.0 collective-permute-done.6.r3
  112.7 0.0 collective-permute-done.5.r2
  112.7 0.0 collective-permute-done.4.r1
  112.7 0.0 copy-done.4
  112.7 0.0 copy-done.5
  112.7 0.0 copy-done.6
  112.7 0.9 shard_map.149
Async XLA Ops:
  2.9 44.6 %copy-start.8 = (s32[1,4,4]{2,1,0:T(4,128)S(1)}, s32[1,4,4]{2,1,0:T(4,128)}, u32[]{:S(2)}) copy-start(s32[1,4,4]{2,1,0:T(4,128)} %param.17) | copy-start | bytes 196
  2.9 44.2 %all-to-all-start = ((bf16[64,64,256]{2,1,0:T(8,128)(2,1)}), bf16[64,64,256]{2,1,0:T(8,128)(2,1)S(1)}, u32[]{:S(2)}, u32[]{:S(2)}) async-start(bf16[64,64,256]{2,1,0:T(8,128)(2,1)} %shard_map.144), calls=%async_computation | async-start | bytes 4194304 | tf_op jit(solution)/shard_map/all_to_all | solution.py:403
  14.9 36.8 %copy-start.2 = (f32[256,256]{1,0:T(8,128)S(1)}, f32[256,256]{1,0:T(8,128)}, u32[]{:S(2)}) copy-start(f32[256,256]{1,0:T(8,128)} %own_heads.1) | copy-start | bytes 786436
  14.9 36.8 %copy-start.3 = (f32[256,256]{1,0:T(8,128)S(1)}, f32[256,256]{1,0:T(8,128)}, u32[]{:S(2)}) copy-start(f32[256,256]{1,0:T(8,128)} %own_tails.1) | copy-start | bytes 786436
  16.9 27.2 %collective-permute-start = (bf16[544,256]{1,0:T(8,128)(2,1)}, bf16[544,256]{1,0:T(8,128)(2,1)S(1)}, u32[]{:S(2)}, u32[]{:S(2)}) collective-permute-start(bf16[544,256]{1,0:T(8,128)(2,1)} %shard_map.145.d0), channel_id=1, source_target_pairs={{0,64},{64,0},{1,65},{65,1},{2,66},{66,2},{3,67},{67,3},{4,68},{68... | collective-permute-start | bytes 835592 | tf_op jit(solution)/shard_map/ppermute | solution.py:349
  18.1 27.9 %collective-permute-start.1 = (bf16[544,256]{1,0:T(8,128)(2,1)}, bf16[544,256]{1,0:T(8,128)(2,1)S(1)}, u32[]{:S(2)}, u32[]{:S(2)}) collective-permute-start(bf16[544,256]{1,0:T(8,128)(2,1)} %shard_map.145.d0), channel_id=1, source_target_pairs={{0,32},{32,0},{1,33},{33,1},{2,34},{34,2},{3,35},{35,3},{4,36},{36... | collective-permute-start | bytes 835592 | tf_op jit(solution)/shard_map/ppermute | solution.py:349
  44.1 3.1 %collective-permute-start.2 = (bf16[544,256]{1,0:T(8,128)(2,1)S(1)}, bf16[544,256]{1,0:T(8,128)(2,1)S(1)}, u32[]{:S(2)}, u32[]{:S(2)}) collective-permute-start(bf16[544,256]{1,0:T(8,128)(2,1)S(1)} %collective-permute-done.d2), channel_id=1, source_target_pairs={{0,32},{32,0},{1,33},{33,1},{2,34},{34,2},{3,35},{35,3},{4,36},{36... | collective-permute-start | bytes 835592 | tf_op jit(solution)/shard_map/ppermute | solution.py:349
  47.1 4.5 %collective-permute-start.3 = (bf16[4096,256]{1,0:T(8,128)(2,1)S(1)}, bf16[4096,256]{1,0:T(8,128)(2,1)}, u32[]{:S(2)}, u32[]{:S(2)}) collective-permute-start(bf16[4096,256]{1,0:T(8,128)(2,1)S(1)} %bitcast.12), channel_id=1, source_target_pairs={{0,32},{32,0},{1,33},{33,1},{2,34},{34,2},{3,35},{35,3},{4,36},{36... | collective-permute-start | bytes 6291464 | tf_op jit(solution)/shard_map/ppermute | solution.py:349
  47.7 1.0 copy-start
  48.6 0.9 copy-start.7
  49.5 2.2 %copy-start.1 = (bf16[544,256]{1,0:T(8,128)(2,1)S(1)}, bf16[544,256]{1,0:T(8,128)(2,1)}, u32[]{:S(2)}) copy-start(bf16[544,256]{1,0:T(8,128)(2,1)} %shard_map.145.d0) | copy-start | bytes 835588
  65.9 46.8 %copy-start.4 = (f32[64,256]{1,0:T(8,128)S(1)}, f32[64,256]{1,0:T(8,128)}, u32[]{:S(2)}) copy-start(f32[64,256]{1,0:T(8,128)} %core.3) | copy-start | bytes 196612
  65.9 46.8 %copy-start.5 = (f32[64,256]{1,0:T(8,128)S(1)}, f32[64,256]{1,0:T(8,128)}, u32[]{:S(2)}) copy-start(f32[64,256]{1,0:T(8,128)} %moment.1) | copy-start | bytes 196612
  66.0 46.8 %copy-start.6 = (f32[64,256]{1,0:T(8,128)S(1)}, f32[64,256]{1,0:T(8,128)}, u32[]{:S(2)}) copy-start(f32[64,256]{1,0:T(8,128)} %second.1) | copy-start | bytes 196612
  96.5 16.2 %collective-permute-start.6 = (f32[32,1408]{1,0:T(8,128)S(1)}, f32[32,1408]{1,0:T(8,128)S(1)}, u32[]{:S(2)}, u32[]{:S(2)}) collective-permute-start(f32[32,1408]{1,0:T(8,128)S(1)} %get-tuple-element.38.r0), channel_id=1, source_target_pairs={{0,96},{32,64},{64,32},{96,0},{1,97},{33,65},{65,33},{97,1},{2,98}... | collective-permute-start | bytes 540680 | tf_op jit(solution)/shard_map/ppermute | solution.py:349
  96.7 16.0 %collective-permute-start.5 = (f32[32,1408]{1,0:T(8,128)S(1)}, f32[32,1408]{1,0:T(8,128)S(1)}, u32[]{:S(2)}, u32[]{:S(2)}) collective-permute-start(f32[32,1408]{1,0:T(8,128)S(1)} %get-tuple-element.38.r0), channel_id=1, source_target_pairs={{0,64},{32,96},{64,0},{96,32},{1,65},{33,97},{65,1},{97,33},{2,66}... | collective-permute-start | bytes 540680 | tf_op jit(solution)/shard_map/ppermute | solution.py:349
  99.6 13.1 %collective-permute-start.4 = (f32[32,1408]{1,0:T(8,128)S(1)}, f32[32,1408]{1,0:T(8,128)S(1)}, u32[]{:S(2)}, u32[]{:S(2)}) collective-permute-start(f32[32,1408]{1,0:T(8,128)S(1)} %get-tuple-element.38.r0), channel_id=1, source_target_pairs={{0,32},{32,0},{64,96},{96,64},{1,33},{33,1},{65,97},{97,65},{2,34}... | collective-permute-start | bytes 540680 | tf_op jit(solution)/shard_map/ppermute | solution.py:349

commit v5 on v4

--- a/solution.py
+++ b/solution.py
@@ -56,17 +56,22 @@
         move.wait()
 
 
-def prepare_kernel(heads, tails, positive, tiles, out_own, hits, names, both, sems):
+def prepare_kernel(
+    heads, tails, positive, tiles, table, out_own, hits, names, both, rows, table_low, sems
+):
     moves = [
         pltpu.make_async_copy(heads, both.at[0:256, :], sems.at[0]),
         pltpu.make_async_copy(tails, both.at[256:512, :], sems.at[1]),
         pltpu.make_async_copy(tiles, names, sems.at[2]),
         pltpu.make_async_copy(positive, hits, sems.at[3]),
+        pltpu.make_async_copy(table, rows, sems.at[4]),
     ]
     for move in moves:
         move.start()
     for move in moves:
         move.wait()
+    table_low[...] = jnp.zeros_like(table_low)
+    table_low[:, 0 : rows.shape[1]] = rows[...].astype(bf16)
     pick = lax.broadcasted_iota(jnp.int32, (8, 8), 0) == lax.broadcasted_iota(
         jnp.int32, (8, 8), 1
     )
@@ -78,6 +83,11 @@
         high = jnp.floor(column * (1.0 / 256.0))
         both[528 + 8 * i : 536 + 8 * i, 0:1] = high
         both[528 + 8 * i : 536 + 8 * i, 1:2] = column - 256.0 * high
+        hot = (
+            column == lax.broadcasted_iota(jnp.int32, (8, REL_PAD), 1).astype(f32)
+        ).astype(f32)
+        hot = jnp.concatenate([hot, jnp.zeros_like(hot)], axis=0).astype(bf16)
+        both[528 + 8 * i : 536 + 8 * i, 128 : 128 + DR] = mm_nt(hot, table_low[...])[0:8]
     out_own[...] = both[...].astype(bf16)
 
 
@@ -96,27 +106,19 @@
     return jnp.concatenate(parts, axis=1).astype(bf16)
 
 
-def form_kernel(mine, d0, d1, d2, d3, table, spread, spread_t, cores, table_low, marks, sems):
-    rel_count = table.shape[1]
+def form_kernel(mine, d0, d1, d2, d3, spread, spread_t, cores, marks, sems):
     moves = [
         pltpu.make_async_copy(d.at[528:544, :], marks.at[s], sems.at[s])
         for s, d in enumerate((d0, d1, d2, d3))
     ]
     for move in moves:
         move.start()
-    table_low[...] = jnp.zeros_like(table_low)
-    table_low[:, 0:rel_count] = table[...].astype(bf16)
     for move in moves:
         move.wait()
-    names = marks[...].reshape(PAIR_ROWS, 256).astype(f32)
-    ids = names[:, 0:1] * 256.0 + names[:, 1:2]
-    hot = (
-        ids == lax.broadcasted_iota(jnp.int32, (PAIR_ROWS, REL_PAD), 1).astype(f32)
-    ).astype(f32).astype(bf16)
-    rel_low = mm_nt(hot, table_low[...]).astype(bf16)
+    rel_low = marks[:, :, 128:256].reshape(PAIR_ROWS, 128)
     copies = (
-        lax.broadcasted_iota(jnp.int32, (DR, 256), 1) % DR
-        == lax.broadcasted_iota(jnp.int32, (DR, 256), 0)
+        lax.broadcasted_iota(jnp.int32, (128, 256), 1) % DR
+        == lax.broadcasted_iota(jnp.int32, (128, 256), 0)
     ).astype(f32).astype(bf16)
     rel_wide = mm(rel_low, copies)
     on_row = on_rows()
@@ -384,19 +386,21 @@
     own = pl.pallas_call(
         prepare_kernel,
         out_shape=jax.ShapeDtypeStruct((544, DE), bf16),
-        in_specs=[pl.BlockSpec(memory_space=pl.ANY)] * 4,
+        in_specs=[pl.BlockSpec(memory_space=pl.ANY)] * 5,
         out_specs=pl.BlockSpec(memory_space=pltpu.VMEM),
         scratch_shapes=[
             pltpu.VMEM((GROUP, 256), jnp.int32),
             pltpu.VMEM((2, 8), jnp.int32),
             pltpu.VMEM((544, DE), f32),
-            pltpu.SemaphoreType.DMA((4,)),
+            pltpu.VMEM((DR, rel_count), f32),
+            pltpu.VMEM((DR, REL_PAD), bf16),
+            pltpu.SemaphoreType.DMA((5,)),
         ],
         compiler_params=pltpu.CompilerParams(vmem_limit_bytes=PREPARE),
         cost_estimate=pl.CostEstimate(
             flops=544 * 256, bytes_accessed=1024 * 1024, transcendentals=0
         ),
-    )(head_vectors, tail_vectors, positive_tail.T, tile_relation)
+    )(head_vectors, tail_vectors, positive_tail.T, tile_relation, relation_table.T)
     across = exchange(own, "xl", 1)
     beside = exchange(own, "co", 1)
 
@@ -412,10 +416,9 @@
             jax.ShapeDtypeStruct((DE, 512), bf16),
             jax.ShapeDtypeStruct((PAIR_ROWS, 128, DE), bf16),
         ),
-        in_specs=vmem(1) + [pl.BlockSpec(memory_space=pl.ANY)] * 4 + vmem(1),
+        in_specs=vmem(1) + [pl.BlockSpec(memory_space=pl.ANY)] * 4,
         out_specs=tuple(vmem(3)),
         scratch_shapes=[
-            pltpu.VMEM((DR, REL_PAD), bf16),
             pltpu.VMEM((GROUP, 16, DE), bf16),
             pltpu.SemaphoreType.DMA((GROUP,)),
         ],
@@ -423,7 +426,7 @@
         cost_estimate=pl.CostEstimate(
             flops=2 * 512 * 256 * 4096, bytes_accessed=8 * 1024 * 1024, transcendentals=0
         ),
-    )(mine, *group, relation_table.T)
+    )(mine, *group)
 
     meta = jnp.concatenate(
         [jnp.stack([member, co, side]).astype(jnp.int32), partner_table.reshape(-1)]

time: 114 us -> 114 us (level)
  transfers between devices with their start and end apart: 8 -> 8, of which waited for: 2 -> 3; matrix products, arithmetic and copies ran while one was open for 0% -> 0% of each run, Pallas kernels for 4% -> 3%
where the time goes in v5:
time: 114 us; the launch traced here: 113 us
  blocking collectives  41.7 us (37%)
  waiting for transfers between devices  26.5 us (23%)
  Pallas kernels  22.8 us (20%)
  starting transfers between devices  20.5 us (18%)
    all_to_all x1, blocking collectives, body(): lax.all_to_all(pay, AXES, split_axis=0, concat_axis=0, tiled=True, axis_i...  28.5 us
    ppermute x7, waiting for transfers between devices, exchange(): return lax.ppermute(value, axes, [(i, i ^ step) for i in range(size)])  26.5 us
    pallas_call x1, Pallas kernels, body(): pl.pallas_call(train_kernel, out_shape=(jax.ShapeDtypeStruct((256, DE), f...  14.2 us
    all_to_all x1, blocking collectives, body(): lax.all_to_all(square, AXES, split_axis=0, concat_axis=0, tiled=True)  13.1 us
    all_to_all x1, starting transfers between devices, body(): lax.all_to_all(low, CHIPS, split_axis=0, concat_axis=0, tiled=True)  12 us
    ppermute x7, starting transfers between devices, exchange(): return lax.ppermute(value, axes, [(i, i ^ step) for i in range(size)])  8.56 us
  transfers between devices with their start and end apart: 8, of which 3 were waited for; matrix products, arithmetic and copies ran while one was open for 0% of the time, Pallas kernels for 3%

profile of v5, /device:TPU:1, one launch (start us, length us, event | category | flops | bytes accessed | tf_op | source)
XLA Modules:
  0.0 113.4 jit_solution(1652019172570181275)
XLA Ops:
  0.6 2.3 %shard_map.144 = bf16[64,64,256]{2,1,0:T(8,128)(2,1)} custom-call(f32[64,256]{1,0:T(8,128)} %core.3), custom_call_target="tpu_custom_call" | custom-call | tf_op jit(solution)/shard_map/pallas_call | solution.py:374
  2.9 0.0 copy-start.7
  2.9 12.0 %all-to-all-start = ((bf16[64,64,256]{2,1,0:T(8,128)(2,1)}), bf16[64,64,256]{2,1,0:T(8,128)(2,1)S(1)}, u32[]{:S(2)}, u32[]{:S(2)}) async-start(bf16[64,64,256]{2,1,0:T(8,128)(2,1)} %shard_map.144), calls=%async_computation | async-start | bytes 4194304 | tf_op jit(solution)/shard_map/all_to_all | solution.py:407
  14.9 0.0 copy-start.2
  14.9 0.0 copy-start.3
  14.9 2.2 %shard_map.145.d0 = bf16[544,256]{1,0:T(8,128)(2,1)} custom-call(f32[256,256]{1,0:T(8,128)} %own_heads.1, f32[256,256]{1,0:T(8,128)} %own_tails.1, s32[4,256]{1,0:T(4,128)} %bitcast.18, s32[2,8]{1,0:T(2,128)} %tiles.1, f32[32,1315]{1,0:T(8,128)} %bitcast.17), custom_call_target="tpu_custom_call" | custom-call | flops 139264 | bytes 1048576 | tf_op jit(solution)/shard_map/pallas_call | solution.py:386
  17.1 1.2 %collective-permute-start = (bf16[544,256]{1,0:T(8,128)(2,1)}, bf16[544,256]{1,0:T(8,128)(2,1)S(1)}, u32[]{:S(2)}, u32[]{:S(2)}) collective-permute-start(bf16[544,256]{1,0:T(8,128)(2,1)} %shard_map.145.d0), channel_id=1, source_target_pairs={{0,64},{64,0},{1,65},{65,1},{2,66},{66,2},{3,67},{67,3},{4,68},{68... | collective-permute-start | bytes 835592 | tf_op jit(solution)/shard_map/ppermute | solution.py:351
  18.3 1.5 %collective-permute-start.1 = (bf16[544,256]{1,0:T(8,128)(2,1)}, bf16[544,256]{1,0:T(8,128)(2,1)S(1)}, u32[]{:S(2)}, u32[]{:S(2)}) collective-permute-start(bf16[544,256]{1,0:T(8,128)(2,1)} %shard_map.145.d0), channel_id=1, source_target_pairs={{0,32},{32,0},{1,33},{33,1},{2,34},{34,2},{3,35},{35,3},{4,36},{36... | collective-permute-start | bytes 835592 | tf_op jit(solution)/shard_map/ppermute | solution.py:351
  19.8 24.3 %collective-permute-done.d2 = bf16[544,256]{1,0:T(8,128)(2,1)S(1)} collective-permute-done((bf16[544,256]{1,0:T(8,128)(2,1)}, bf16[544,256]{1,0:T(8,128)(2,1)S(1)}, u32[]{:S(2)}, u32[]{:S(2)}) %collective-permute-start) | collective-permute-done | bytes 278560 | tf_op jit(solution)/shard_map/ppermute | solution.py:351
  44.1 1.9 %collective-permute-start.2 = (bf16[544,256]{1,0:T(8,128)(2,1)S(1)}, bf16[544,256]{1,0:T(8,128)(2,1)S(1)}, u32[]{:S(2)}, u32[]{:S(2)}) collective-permute-start(bf16[544,256]{1,0:T(8,128)(2,1)S(1)} %collective-permute-done.d2), channel_id=1, source_target_pairs={{0,32},{32,0},{1,33},{33,1},{2,34},{34,2},{3,35},{35,3},{4,36},{36... | collective-permute-start | bytes 835592 | tf_op jit(solution)/shard_map/ppermute | solution.py:351
  45.9 0.0 collective-permute-done.1.d1
  45.9 1.2 %collective-permute-done.2.d3 = bf16[544,256]{1,0:T(8,128)(2,1)S(1)} collective-permute-done((bf16[544,256]{1,0:T(8,128)(2,1)S(1)}, bf16[544,256]{1,0:T(8,128)(2,1)S(1)}, u32[]{:S(2)}, u32[]{:S(2)}) %collective-permute-start.2) | collective-permute-done | bytes 278560 | tf_op jit(solution)/shard_map/ppermute | solution.py:351
  47.1 0.0 all-to-all-done
  47.1 0.4 collective-permute-start.3
  47.5 0.0 copy-done.7
  47.5 0.1 reshape.22
  47.6 0.1 pad_add_fusion.meta
  47.7 0.0 copy-start
  47.7 1.0 copy-done
  48.6 0.0 copy-start.1
  48.6 1.8 %shard_map.146 = (bf16[512,256]{1,0:T(8,128)(2,1)S(1)}, bf16[256,512]{1,0:T(8,128)(2,1)S(1)}, bf16[64,128,256]{2,1,0:T(8,128)(2,1)S(1)}) custom-call(bf16[4096,256]{1,0:T(8,128)(2,1)S(1)} %bitcast.13, bf16[544,256]{1,0:T(8,128)(2,1)S(1)} %copy-done, bf16[544,256]{1,0:T(8,128)(2,1)S(1)} %collective-permute-done.1.d1, ...), custom_call_target="tpu_custom_call" | custom-call | flops 1073741824 | bytes 8388608 | tf_op jit(solution)/shard_map/pallas_call | solution.py:412
  50.4 1.0 collective-permute-done.3.other
  51.4 0.0 copy-done.2
  51.4 0.0 copy-done.3
  51.4 0.0 copy-done.1
  51.4 14.2 %shard_map.147 = (f32[256,256]{1,0:T(8,128)}, f32[256,256]{1,0:T(8,128)}, f32[4,256]{1,0:T(4,128)}, bf16[32,80,256]{2,1,0:T(8,128)(2,1)S(1)}) custom-call(s32[19]{0:T(128)S(1)} %pad_add_fusion.meta, bf16[4096,256]{1,0:T(8,128)(2,1)S(1)} %bitcast.14, bf16[4096,256]{1,0:T(8,128)(2,1)} %collective-permute-done.3.other, f32[256,256]{1,0:T(8,128)S(1)} %copy-done.2, ...), custom_call_target="tpu_custom_call" | custom-call | tf_op jit(solution)/shard_map/pallas_call | solution.py:434
  65.6 0.0 copy-start.4
  65.7 0.0 copy-start.5
  65.7 0.0 copy-start.6
  65.7 28.5 %all_to_all.21.got = bf16[32,80,256]{2,1,0:T(8,128)(2,1)S(1)} all-to-all(bf16[32,80,256]{2,1,0:T(8,128)(2,1)S(1)} %get-tuple-element.35), channel_id=1, replica_groups={{0,1,2,3,8,9,10,11,16,17,18,19,24,25,26,27,68,69,70,71,76,77,78,79,84,8..., dimensions={0} | all-to-all | bytes 2621440 | tf_op jit(solution)/shard_map/all_to_all | solution.py:467
  94.2 1.5 %shard_map.148 = (f32[64,256]{1,0:T(8,128)S(1)}, f32[128,128]{1,0:T(8,128)S(1)}, f32[32,1408]{1,0:T(8,128)S(1)}) custom-call(bf16[32,80,256]{2,1,0:T(8,128)(2,1)S(1)} %all_to_all.21.got), custom_call_target="tpu_custom_call" | custom-call | tf_op jit(solution)/shard_map/pallas_call | solution.py:470
  95.7 0.8 collective-permute-start.6
  96.4 2.9 %collective-permute-start.5 = (f32[32,1408]{1,0:T(8,128)S(1)}, f32[32,1408]{1,0:T(8,128)S(1)}, u32[]{:S(2)}, u32[]{:S(2)}) collective-permute-start(f32[32,1408]{1,0:T(8,128)S(1)} %get-tuple-element.38.r0), channel_id=1, source_target_pairs={{0,64},{32,96},{64,0},{96,32},{1,65},{33,97},{65,1},{97,33},{2,66}... | collective-permute-start | bytes 540680 | tf_op jit(solution)/shard_map/ppermute | solution.py:351
  99.3 0.0 collective-permute-start.4
  99.3 13.1 %all_to_all.22 = f32[128,1,128]{2,1,0:T(1,128)S(1)} all-to-all(f32[128,1,128]{2,1,0:T(1,128)S(1)} %bitcast.16), channel_id=1, replica_groups=mesh['xl'=2,'co'=2,'z'=4,'xh'=2,'y'=4] {'xl','co','z','xh','y'}, dimensions={0} | all-to-all | bytes 131072 | tf_op jit(solution)/shard_map/all_to_all | solution.py:482
  112.4 0.0 collective-permute-done.6.r3
  112.4 0.0 collective-permute-done.5.r2
  112.4 0.0 collective-permute-done.4.r1
  112.4 0.0 copy-done.4
  112.4 0.0 copy-done.5
  112.4 0.0 copy-done.6
  112.5 0.9 shard_map.149
Async XLA Ops:
  2.9 44.6 %copy-start.7 = (s32[1,4,4]{2,1,0:T(4,128)S(1)}, s32[1,4,4]{2,1,0:T(4,128)}, u32[]{:S(2)}) copy-start(s32[1,4,4]{2,1,0:T(4,128)} %param.17) | copy-start | bytes 196
  2.9 44.2 %all-to-all-start = ((bf16[64,64,256]{2,1,0:T(8,128)(2,1)}), bf16[64,64,256]{2,1,0:T(8,128)(2,1)S(1)}, u32[]{:S(2)}, u32[]{:S(2)}) async-start(bf16[64,64,256]{2,1,0:T(8,128)(2,1)} %shard_map.144), calls=%async_computation | async-start | bytes 4194304 | tf_op jit(solution)/shard_map/all_to_all | solution.py:407
  14.9 36.5 %copy-start.2 = (f32[256,256]{1,0:T(8,128)S(1)}, f32[256,256]{1,0:T(8,128)}, u32[]{:S(2)}) copy-start(f32[256,256]{1,0:T(8,128)} %own_heads.1) | copy-start | bytes 786436
  14.9 36.5 %copy-start.3 = (f32[256,256]{1,0:T(8,128)S(1)}, f32[256,256]{1,0:T(8,128)}, u32[]{:S(2)}) copy-start(f32[256,256]{1,0:T(8,128)} %own_tails.1) | copy-start | bytes 786436
  17.1 27.0 %collective-permute-start = (bf16[544,256]{1,0:T(8,128)(2,1)}, bf16[544,256]{1,0:T(8,128)(2,1)S(1)}, u32[]{:S(2)}, u32[]{:S(2)}) collective-permute-start(bf16[544,256]{1,0:T(8,128)(2,1)} %shard_map.145.d0), channel_id=1, source_target_pairs={{0,64},{64,0},{1,65},{65,1},{2,66},{66,2},{3,67},{67,3},{4,68},{68... | collective-permute-start | bytes 835592 | tf_op jit(solution)/shard_map/ppermute | solution.py:351
  18.3 27.7 %collective-permute-start.1 = (bf16[544,256]{1,0:T(8,128)(2,1)}, bf16[544,256]{1,0:T(8,128)(2,1)S(1)}, u32[]{:S(2)}, u32[]{:S(2)}) collective-permute-start(bf16[544,256]{1,0:T(8,128)(2,1)} %shard_map.145.d0), channel_id=1, source_target_pairs={{0,32},{32,0},{1,33},{33,1},{2,34},{34,2},{3,35},{35,3},{4,36},{36... | collective-permute-start | bytes 835592 | tf_op jit(solution)/shard_map/ppermute | solution.py:351
  44.1 3.1 %collective-permute-start.2 = (bf16[544,256]{1,0:T(8,128)(2,1)S(1)}, bf16[544,256]{1,0:T(8,128)(2,1)S(1)}, u32[]{:S(2)}, u32[]{:S(2)}) collective-permute-start(bf16[544,256]{1,0:T(8,128)(2,1)S(1)} %collective-permute-done.d2), channel_id=1, source_target_pairs={{0,32},{32,0},{1,33},{33,1},{2,34},{34,2},{3,35},{35,3},{4,36},{36... | collective-permute-start | bytes 835592 | tf_op jit(solution)/shard_map/ppermute | solution.py:351
  47.1 4.3 %collective-permute-start.3 = (bf16[4096,256]{1,0:T(8,128)(2,1)S(1)}, bf16[4096,256]{1,0:T(8,128)(2,1)}, u32[]{:S(2)}, u32[]{:S(2)}) collective-permute-start(bf16[4096,256]{1,0:T(8,128)(2,1)S(1)} %bitcast.12), channel_id=1, source_target_pairs={{0,32},{32,0},{1,33},{33,1},{2,34},{34,2},{3,35},{35,3},{4,36},{36... | collective-permute-start | bytes 6291464 | tf_op jit(solution)/shard_map/ppermute | solution.py:351
  47.7 1.0 copy-start
  48.6 2.8 %copy-start.1 = (bf16[544,256]{1,0:T(8,128)(2,1)S(1)}, bf16[544,256]{1,0:T(8,128)(2,1)}, u32[]{:S(2)}) copy-start(bf16[544,256]{1,0:T(8,128)(2,1)} %shard_map.145.d0) | copy-start | bytes 835588
  65.6 46.8 %copy-start.4 = (f32[64,256]{1,0:T(8,128)S(1)}, f32[64,256]{1,0:T(8,128)}, u32[]{:S(2)}) copy-start(f32[64,256]{1,0:T(8,128)} %core.3) | copy-start | bytes 196612
  65.7 46.8 %copy-start.5 = (f32[64,256]{1,0:T(8,128)S(1)}, f32[64,256]{1,0:T(8,128)}, u32[]{:S(2)}) copy-start(f32[64,256]{1,0:T(8,128)} %moment.1) | copy-start | bytes 196612
  65.7 46.8 %copy-start.6 = (f32[64,256]{1,0:T(8,128)S(1)}, f32[64,256]{1,0:T(8,128)}, u32[]{:S(2)}) copy-start(f32[64,256]{1,0:T(8,128)} %second.1) | copy-start | bytes 196612
  95.7 16.8 %collective-permute-start.6 = (f32[32,1408]{1,0:T(8,128)S(1)}, f32[32,1408]{1,0:T(8,128)S(1)}, u32[]{:S(2)}, u32[]{:S(2)}) collective-permute-start(f32[32,1408]{1,0:T(8,128)S(1)} %get-tuple-element.38.r0), channel_id=1, source_target_pairs={{0,96},{32,64},{64,32},{96,0},{1,97},{33,65},{65,33},{97,1},{2,98}... | collective-permute-start | bytes 540680 | tf_op jit(solution)/shard_map/ppermute | solution.py:351
  96.4 16.0 %collective-permute-start.5 = (f32[32,1408]{1,0:T(8,128)S(1)}, f32[32,1408]{1,0:T(8,128)S(1)}, u32[]{:S(2)}, u32[]{:S(2)}) collective-permute-start(f32[32,1408]{1,0:T(8,128)S(1)} %get-tuple-element.38.r0), channel_id=1, source_target_pairs={{0,64},{32,96},{64,0},{96,32},{1,65},{33,97},{65,1},{97,33},{2,66}... | collective-permute-start | bytes 540680 | tf_op jit(solution)/shard_map/ppermute | solution.py:351
  99.3 13.1 %collective-permute-start.4 = (f32[32,1408]{1,0:T(8,128)S(1)}, f32[32,1408]{1,0:T(8,128)S(1)}, u32[]{:S(2)}, u32[]{:S(2)}) collective-permute-start(f32[32,1408]{1,0:T(8,128)S(1)} %get-tuple-element.38.r0), channel_id=1, source_target_pairs={{0,32},{32,0},{64,96},{96,64},{1,33},{33,1},{65,97},{97,65},{2,34}... | collective-permute-start | bytes 540680 | tf_op jit(solution)/shard_map/ppermute | solution.py:351

commit v6 on v5

--- a/solution.py
+++ b/solution.py
@@ -126,7 +126,7 @@
     spread[...] = spread_f.astype(bf16)
     spread_t[...] = spread_f.T.astype(bf16)
 
-    @pl.loop(0, 8, unroll=4)
+    @pl.loop(0, 8, unroll=8)
     def _(q):
         cores[:, pl.ds(pl.multiple_of(16 * q, 16), 16), :] = core_step(spread, mine, q)
 
@@ -179,7 +179,7 @@
         cores[:, pl.ds(at, 64), :] = formed[:, 64 * x : 64 * x + 64, :]
     fetch_other.wait()
 
-    @pl.loop(0, 8, unroll=4)
+    @pl.loop(0, 8, unroll=8)
     def _(q):
         at = 64 * (2 * (q // 4) + 1 - co) + 16 * (q % 4)
         cores[:, pl.ds(pl.multiple_of(at, 16), 16), :] = core_step(spread, other_here, q)

time: 114 us -> 114 us (level)
  no operation moved by 1% of the time
where the time goes in v6:
time: 114 us; the launch traced here: 113 us
  blocking collectives  41.7 us (37%)
  waiting for transfers between devices  26.8 us (24%)
  Pallas kernels  22.3 us (20%)
  starting transfers between devices  20.5 us (18%)
    all_to_all x1, blocking collectives, body(): lax.all_to_all(pay, AXES, split_axis=0, concat_axis=0, tiled=True, axis_i...  28.6 us
    ppermute x7, waiting for transfers between devices, exchange(): return lax.ppermute(value, axes, [(i, i ^ step) for i in range(size)])  26.8 us
    pallas_call x1, Pallas kernels, body(): pl.pallas_call(train_kernel, out_shape=(jax.ShapeDtypeStruct((256, DE), f...  14.1 us
    all_to_all x1, blocking collectives, body(): lax.all_to_all(square, AXES, split_axis=0, concat_axis=0, tiled=True)  13.1 us
    all_to_all x1, starting transfers between devices, body(): lax.all_to_all(low, CHIPS, split_axis=0, concat_axis=0, tiled=True)  12 us
    ppermute x7, starting transfers between devices, exchange(): return lax.ppermute(value, axes, [(i, i ^ step) for i in range(size)])  8.53 us
  transfers between devices with their start and end apart: 8, of which 3 were waited for; matrix products, arithmetic and copies ran while one was open for 0% of the time, Pallas kernels for 3%

profile of v6, /device:TPU:1, one launch (start us, length us, event | category | flops | bytes accessed | tf_op | source)
XLA Modules:
  0.0 113.2 jit_solution(15782768224786509130)
XLA Ops:
  0.6 2.3 %shard_map.144 = bf16[64,64,256]{2,1,0:T(8,128)(2,1)} custom-call(f32[64,256]{1,0:T(8,128)} %core.3), custom_call_target="tpu_custom_call" | custom-call | tf_op jit(solution)/shard_map/pallas_call | solution.py:374
  2.9 0.0 copy-start.7
  2.9 12.0 %all-to-all-start = ((bf16[64,64,256]{2,1,0:T(8,128)(2,1)}), bf16[64,64,256]{2,1,0:T(8,128)(2,1)S(1)}, u32[]{:S(2)}, u32[]{:S(2)}) async-start(bf16[64,64,256]{2,1,0:T(8,128)(2,1)} %shard_map.144), calls=%async_computation | async-start | bytes 4194304 | tf_op jit(solution)/shard_map/all_to_all | solution.py:407
  14.9 0.0 copy-start.2
  14.9 0.0 copy-start.3
  14.9 2.2 %shard_map.145.d0 = bf16[544,256]{1,0:T(8,128)(2,1)} custom-call(f32[256,256]{1,0:T(8,128)} %own_heads.1, f32[256,256]{1,0:T(8,128)} %own_tails.1, s32[4,256]{1,0:T(4,128)} %bitcast.18, s32[2,8]{1,0:T(2,128)} %tiles.1, f32[32,1315]{1,0:T(8,128)} %bitcast.17), custom_call_target="tpu_custom_call" | custom-call | flops 139264 | bytes 1048576 | tf_op jit(solution)/shard_map/pallas_call | solution.py:386
  17.1 1.2 %collective-permute-start = (bf16[544,256]{1,0:T(8,128)(2,1)}, bf16[544,256]{1,0:T(8,128)(2,1)S(1)}, u32[]{:S(2)}, u32[]{:S(2)}) collective-permute-start(bf16[544,256]{1,0:T(8,128)(2,1)} %shard_map.145.d0), channel_id=1, source_target_pairs={{0,64},{64,0},{1,65},{65,1},{2,66},{66,2},{3,67},{67,3},{4,68},{68... | collective-permute-start | bytes 835592 | tf_op jit(solution)/shard_map/ppermute | solution.py:351
  18.3 1.5 %collective-permute-start.1 = (bf16[544,256]{1,0:T(8,128)(2,1)}, bf16[544,256]{1,0:T(8,128)(2,1)S(1)}, u32[]{:S(2)}, u32[]{:S(2)}) collective-permute-start(bf16[544,256]{1,0:T(8,128)(2,1)} %shard_map.145.d0), channel_id=1, source_target_pairs={{0,32},{32,0},{1,33},{33,1},{2,34},{34,2},{3,35},{35,3},{4,36},{36... | collective-permute-start | bytes 835592 | tf_op jit(solution)/shard_map/ppermute | solution.py:351
  19.8 24.3 %collective-permute-done.d2 = bf16[544,256]{1,0:T(8,128)(2,1)S(1)} collective-permute-done((bf16[544,256]{1,0:T(8,128)(2,1)}, bf16[544,256]{1,0:T(8,128)(2,1)S(1)}, u32[]{:S(2)}, u32[]{:S(2)}) %collective-permute-start) | collective-permute-done | bytes 278560 | tf_op jit(solution)/shard_map/ppermute | solution.py:351
  44.1 1.9 %collective-permute-start.2 = (bf16[544,256]{1,0:T(8,128)(2,1)S(1)}, bf16[544,256]{1,0:T(8,128)(2,1)S(1)}, u32[]{:S(2)}, u32[]{:S(2)}) collective-permute-start(bf16[544,256]{1,0:T(8,128)(2,1)S(1)} %collective-permute-done.d2), channel_id=1, source_target_pairs={{0,32},{32,0},{1,33},{33,1},{2,34},{34,2},{3,35},{35,3},{4,36},{36... | collective-permute-start | bytes 835592 | tf_op jit(solution)/shard_map/ppermute | solution.py:351
  45.9 0.0 collective-permute-done.1.d1
  45.9 1.2 %collective-permute-done.2.d3 = bf16[544,256]{1,0:T(8,128)(2,1)S(1)} collective-permute-done((bf16[544,256]{1,0:T(8,128)(2,1)S(1)}, bf16[544,256]{1,0:T(8,128)(2,1)S(1)}, u32[]{:S(2)}, u32[]{:S(2)}) %collective-permute-start.2) | collective-permute-done | bytes 278560 | tf_op jit(solution)/shard_map/ppermute | solution.py:351
  47.1 0.0 all-to-all-done
  47.1 0.4 collective-permute-start.3
  47.5 0.0 copy-done.7
  47.5 0.1 reshape.22
  47.6 0.1 pad_add_fusion.meta
  47.7 0.0 copy-start
  47.7 1.0 copy-done
  48.6 0.0 copy-start.1
  48.6 1.4 %shard_map.146 = (bf16[512,256]{1,0:T(8,128)(2,1)S(1)}, bf16[256,512]{1,0:T(8,128)(2,1)S(1)}, bf16[64,128,256]{2,1,0:T(8,128)(2,1)S(1)}) custom-call(bf16[4096,256]{1,0:T(8,128)(2,1)S(1)} %bitcast.13, bf16[544,256]{1,0:T(8,128)(2,1)S(1)} %copy-done, bf16[544,256]{1,0:T(8,128)(2,1)S(1)} %collective-permute-done.1.d1, ...), custom_call_target="tpu_custom_call" | custom-call | flops 1073741824 | bytes 8388608 | tf_op jit(solution)/shard_map/pallas_call | solution.py:412
  50.1 1.3 %collective-permute-done.3.other = bf16[4096,256]{1,0:T(8,128)(2,1)} collective-permute-done((bf16[4096,256]{1,0:T(8,128)(2,1)S(1)}, bf16[4096,256]{1,0:T(8,128)(2,1)}, u32[]{:S(2)}, u32[]{:S(2)}) %collective-permute-start.3) | collective-permute-done | bytes 2097184 | tf_op jit(solution)/shard_map/ppermute | solution.py:351
  51.4 0.0 copy-done.2
  51.4 0.0 copy-done.3
  51.4 0.0 copy-done.1
  51.4 14.1 %shard_map.147 = (f32[256,256]{1,0:T(8,128)}, f32[256,256]{1,0:T(8,128)}, f32[4,256]{1,0:T(4,128)}, bf16[32,80,256]{2,1,0:T(8,128)(2,1)S(1)}) custom-call(s32[19]{0:T(128)S(1)} %pad_add_fusion.meta, bf16[4096,256]{1,0:T(8,128)(2,1)S(1)} %bitcast.14, bf16[4096,256]{1,0:T(8,128)(2,1)} %collective-permute-done.3.other, f32[256,256]{1,0:T(8,128)S(1)} %copy-done.2, ...), custom_call_target="tpu_custom_call" | custom-call | tf_op jit(solution)/shard_map/pallas_call | solution.py:434
  65.5 0.0 copy-start.4
  65.5 0.0 copy-start.5
  65.5 0.0 copy-start.6
  65.5 28.6 %all_to_all.21.got = bf16[32,80,256]{2,1,0:T(8,128)(2,1)S(1)} all-to-all(bf16[32,80,256]{2,1,0:T(8,128)(2,1)S(1)} %get-tuple-element.35), channel_id=1, replica_groups={{0,1,2,3,8,9,10,11,16,17,18,19,24,25,26,27,68,69,70,71,76,77,78,79,84,8..., dimensions={0} | all-to-all | bytes 2621440 | tf_op jit(solution)/shard_map/all_to_all | solution.py:467
  94.1 1.5 %shard_map.148 = (f32[64,256]{1,0:T(8,128)S(1)}, f32[128,128]{1,0:T(8,128)S(1)}, f32[32,1408]{1,0:T(8,128)S(1)}) custom-call(bf16[32,80,256]{2,1,0:T(8,128)(2,1)S(1)} %all_to_all.21.got), custom_call_target="tpu_custom_call" | custom-call | tf_op jit(solution)/shard_map/pallas_call | solution.py:470
  95.5 0.7 collective-permute-start.6
  96.2 2.9 %collective-permute-start.5 = (f32[32,1408]{1,0:T(8,128)S(1)}, f32[32,1408]{1,0:T(8,128)S(1)}, u32[]{:S(2)}, u32[]{:S(2)}) collective-permute-start(f32[32,1408]{1,0:T(8,128)S(1)} %get-tuple-element.38.r0), channel_id=1, source_target_pairs={{0,64},{32,96},{64,0},{96,32},{1,65},{33,97},{65,1},{97,33},{2,66}... | collective-permute-start | bytes 540680 | tf_op jit(solution)/shard_map/ppermute | solution.py:351
  99.1 0.0 collective-permute-start.4
  99.1 13.1 %all_to_all.22 = f32[128,1,128]{2,1,0:T(1,128)S(1)} all-to-all(f32[128,1,128]{2,1,0:T(1,128)S(1)} %bitcast.16), channel_id=1, replica_groups=mesh['xl'=2,'co'=2,'z'=4,'xh'=2,'y'=4] {'xl','co','z','xh','y'}, dimensions={0} | all-to-all | bytes 131072 | tf_op jit(solution)/shard_map/all_to_all | solution.py:482
  112.3 0.0 collective-permute-done.6.r3
  112.3 0.0 collective-permute-done.5.r2
  112.3 0.0 collective-permute-done.4.r1
  112.3 0.0 copy-done.4
  112.3 0.0 copy-done.5
  112.3 0.0 copy-done.6
  112.3 0.9 shard_map.149
Async XLA Ops:
  2.9 44.6 %copy-start.7 = (s32[1,4,4]{2,1,0:T(4,128)S(1)}, s32[1,4,4]{2,1,0:T(4,128)}, u32[]{:S(2)}) copy-start(s32[1,4,4]{2,1,0:T(4,128)} %param.17) | copy-start | bytes 196
  2.9 44.2 %all-to-all-start = ((bf16[64,64,256]{2,1,0:T(8,128)(2,1)}), bf16[64,64,256]{2,1,0:T(8,128)(2,1)S(1)}, u32[]{:S(2)}, u32[]{:S(2)}) async-start(bf16[64,64,256]{2,1,0:T(8,128)(2,1)} %shard_map.144), calls=%async_computation | async-start | bytes 4194304 | tf_op jit(solution)/shard_map/all_to_all | solution.py:407
  14.9 36.5 %copy-start.2 = (f32[256,256]{1,0:T(8,128)S(1)}, f32[256,256]{1,0:T(8,128)}, u32[]{:S(2)}) copy-start(f32[256,256]{1,0:T(8,128)} %own_heads.1) | copy-start | bytes 786436
  14.9 36.5 %copy-start.3 = (f32[256,256]{1,0:T(8,128)S(1)}, f32[256,256]{1,0:T(8,128)}, u32[]{:S(2)}) copy-start(f32[256,256]{1,0:T(8,128)} %own_tails.1) | copy-start | bytes 786436
  17.1 27.0 %collective-permute-start = (bf16[544,256]{1,0:T(8,128)(2,1)}, bf16[544,256]{1,0:T(8,128)(2,1)S(1)}, u32[]{:S(2)}, u32[]{:S(2)}) collective-permute-start(bf16[544,256]{1,0:T(8,128)(2,1)} %shard_map.145.d0), channel_id=1, source_target_pairs={{0,64},{64,0},{1,65},{65,1},{2,66},{66,2},{3,67},{67,3},{4,68},{68... | collective-permute-start | bytes 835592 | tf_op jit(solution)/shard_map/ppermute | solution.py:351
  18.3 27.7 %collective-permute-start.1 = (bf16[544,256]{1,0:T(8,128)(2,1)}, bf16[544,256]{1,0:T(8,128)(2,1)S(1)}, u32[]{:S(2)}, u32[]{:S(2)}) collective-permute-start(bf16[544,256]{1,0:T(8,128)(2,1)} %shard_map.145.d0), channel_id=1, source_target_pairs={{0,32},{32,0},{1,33},{33,1},{2,34},{34,2},{3,35},{35,3},{4,36},{36... | collective-permute-start | bytes 835592 | tf_op jit(solution)/shard_map/ppermute | solution.py:351
  44.1 3.1 %collective-permute-start.2 = (bf16[544,256]{1,0:T(8,128)(2,1)S(1)}, bf16[544,256]{1,0:T(8,128)(2,1)S(1)}, u32[]{:S(2)}, u32[]{:S(2)}) collective-permute-start(bf16[544,256]{1,0:T(8,128)(2,1)S(1)} %collective-permute-done.d2), channel_id=1, source_target_pairs={{0,32},{32,0},{1,33},{33,1},{2,34},{34,2},{3,35},{35,3},{4,36},{36... | collective-permute-start | bytes 835592 | tf_op jit(solution)/shard_map/ppermute | solution.py:351
  47.1 4.3 %collective-permute-start.3 = (bf16[4096,256]{1,0:T(8,128)(2,1)S(1)}, bf16[4096,256]{1,0:T(8,128)(2,1)}, u32[]{:S(2)}, u32[]{:S(2)}) collective-permute-start(bf16[4096,256]{1,0:T(8,128)(2,1)S(1)} %bitcast.12), channel_id=1, source_target_pairs={{0,32},{32,0},{1,33},{33,1},{2,34},{34,2},{3,35},{35,3},{4,36},{36... | collective-permute-start | bytes 6291464 | tf_op jit(solution)/shard_map/ppermute | solution.py:351
  47.7 1.0 copy-start
  48.6 2.8 %copy-start.1 = (bf16[544,256]{1,0:T(8,128)(2,1)S(1)}, bf16[544,256]{1,0:T(8,128)(2,1)}, u32[]{:S(2)}) copy-start(bf16[544,256]{1,0:T(8,128)(2,1)} %shard_map.145.d0) | copy-start | bytes 835588
  65.5 46.8 %copy-start.4 = (f32[64,256]{1,0:T(8,128)S(1)}, f32[64,256]{1,0:T(8,128)}, u32[]{:S(2)}) copy-start(f32[64,256]{1,0:T(8,128)} %core.3) | copy-start | bytes 196612
  65.5 46.8 %copy-start.5 = (f32[64,256]{1,0:T(8,128)S(1)}, f32[64,256]{1,0:T(8,128)}, u32[]{:S(2)}) copy-start(f32[64,256]{1,0:T(8,128)} %moment.1) | copy-start | bytes 196612
  65.5 46.8 %copy-start.6 = (f32[64,256]{1,0:T(8,128)S(1)}, f32[64,256]{1,0:T(8,128)}, u32[]{:S(2)}) copy-start(f32[64,256]{1,0:T(8,128)} %second.1) | copy-start | bytes 196612
  95.5 16.7 %collective-permute-start.6 = (f32[32,1408]{1,0:T(8,128)S(1)}, f32[32,1408]{1,0:T(8,128)S(1)}, u32[]{:S(2)}, u32[]{:S(2)}) collective-permute-start(f32[32,1408]{1,0:T(8,128)S(1)} %get-tuple-element.38.r0), channel_id=1, source_target_pairs={{0,96},{32,64},{64,32},{96,0},{1,97},{33,65},{65,33},{97,1},{2,98}... | collective-permute-start | bytes 540680 | tf_op jit(solution)/shard_map/ppermute | solution.py:351
  96.2 16.0 %collective-permute-start.5 = (f32[32,1408]{1,0:T(8,128)S(1)}, f32[32,1408]{1,0:T(8,128)S(1)}, u32[]{:S(2)}, u32[]{:S(2)}) collective-permute-start(f32[32,1408]{1,0:T(8,128)S(1)} %get-tuple-element.38.r0), channel_id=1, source_target_pairs={{0,64},{32,96},{64,0},{96,32},{1,65},{33,97},{65,1},{97,33},{2,66}... | collective-permute-start | bytes 540680 | tf_op jit(solution)/shard_map/ppermute | solution.py:351
  99.1 13.1 %collective-permute-start.4 = (f32[32,1408]{1,0:T(8,128)S(1)}, f32[32,1408]{1,0:T(8,128)S(1)}, u32[]{:S(2)}, u32[]{:S(2)}) collective-permute-start(f32[32,1408]{1,0:T(8,128)S(1)} %get-tuple-element.38.r0), channel_id=1, source_target_pairs={{0,32},{32,0},{64,96},{96,64},{1,33},{33,1},{65,97},{97,65},{2,34}... | collective-permute-start | bytes 540680 | tf_op jit(solution)/shard_map/ppermute | solution.py:351
